TPU v7x, 128 devices: a whole 4x4x4 slice. The times are simulated.
128 devices in a mesh: wide: 64 (over x, z_lo, y, core), narrow: 2 (over z_hi).
Axes of the slice: x: 4, y: 4, z: 4 (z_hi: 2, z_lo: 2; z = z_hi * 2 + z_lo), core: 2. Of those that a mesh axis runs over, the one named last changes fastest.
Arguments:
- tests: float32 [1024, 32, 3, 8, 64], P('wide', None, None, 'narrow'), may hold values from -6 to 6
- block_inverse: float32 [1024, 3, 3, 8, 64], P('wide', None, None, 'narrow'), may hold values from -0.25 to 0.4, as said below
- face_weight: float32 [1024, 6, 8, 64], P('wide', None, 'narrow'), may hold values from 0.3 to 1
- mixing: float32 [6, 3, 3], replicated, may hold values from -3 to 3
- far_tiles: bfloat16 [1024, 2, 3, 256, 256], P('wide', 'narrow'), may hold values from -0.21875 to 0.21875
- far_column: int32 [1024, 2, 3], P('wide', 'narrow'), may hold values from 0 to 15
- aggregate: int32 [1024, 8, 64], P('wide', 'narrow'), may hold values from 0 to 127, as said below
- owner_map: int32 [8192], P(('wide', 'narrow')), may hold values from 0 to 127, as said below
Outputs:
- prolong: float32 [1024, 32, 3, 8, 64], P('wide', None, None, 'narrow')
- coarse_basis: float32 [128, 256, 1024], P(('wide', 'narrow'))
Inputs may be any that keep to these rules, and one draw needn't show every extreme that they name: `aggregate`: aggregate numbers of the nodes of one wide rank; every number of a wide rank is used. `owner_map`: no home device has more than 2 aggregates with the same owner; in every draw some owner receives 2 aggregates from every home device. `block_inverse`: diagonal entries lie in 0.2 to 0.4.
All inputs are finite; a program needn't handle non-finite values.
Results may differ from a plain program's by a relative error of at most 0.0022.
Values may be sent and summed in bfloat16 or wider, within the bound.
A program may use at most 128 MiB of HBM per device.

v0:
```python
import jax
import jax.numpy as jnp
from jax import lax
from jax.sharding import PartitionSpec as P

SWEEPS = 3
SLOT = 2


omega_relax = 0.5
ridge_shift = 0.001
highest = lax.Precision.HIGHEST


def with_halo(x, sides, width):
    for axis, dim in sides:
        size, length = (lax.axis_size(axis), x.shape[dim])
        up = [(i, (i + 1) % size) for i in range(size - 1)]
        down = [(j, i) for i, j in up]
        last = lax.slice_in_dim(x, length - width, length, axis=dim)
        first = lax.slice_in_dim(x, 0, width, axis=dim)
        before = lax.ppermute(last, axis, up)
        after = lax.ppermute(first, axis, down)
        x = jnp.concatenate([before, x, after], axis=dim)
    return x


def shifted_2(x, axis, by):
    size = lax.axis_size(axis)
    return lax.ppermute(x, axis, [(i, (i + by) % size) for i in range(size)])


def mix_components(matrix, field_values):
    return jnp.stack(
        [
            matrix[component, 0] * field_values[:, :, 0]
            + matrix[component, 1] * field_values[:, :, 1]
            + matrix[component, 2] * field_values[:, :, 2]
            for component in range(3)
        ],
        axis=2,
    )


def relax_step(field_values, padded, block_inverse, face_weight, mixing):
    zero_face = jnp.zeros_like(field_values[..., :1])
    neighbours = [
        padded[2:, :, :, 1:-1],
        padded[:-2, :, :, 1:-1],
        padded[1:-1, :, :, 2:],
        padded[1:-1, :, :, :-2],
        jnp.concatenate([field_values[..., 1:], zero_face], axis=4),
        jnp.concatenate([zero_face, field_values[..., :-1]], axis=4),
    ]
    coupled = face_weight[:, 0][:, None, None] * mix_components(mixing[0], neighbours[0])
    for direction in range(1, 6):
        coupled = coupled + face_weight[:, direction][:, None, None] * mix_components(
            mixing[direction], neighbours[direction]
        )
    jacobi = jnp.stack(
        [
            block_inverse[:, component, 0][:, None] * coupled[:, :, 0]
            + block_inverse[:, component, 1][:, None] * coupled[:, :, 1]
            + block_inverse[:, component, 2][:, None] * coupled[:, :, 2]
            for component in range(3)
        ],
        axis=2,
    )
    return (1.0 - omega_relax) * field_values + omega_relax * jacobi


def factorize(matrices):
    order = matrices.shape[1]
    source = jnp.transpose(matrices, (1, 2, 0))
    row_ids = jnp.arange(order, dtype=jnp.int32)
    factor = jnp.zeros_like(source)
    for column in range(order):
        column_values = source[:, column, :] - jnp.sum(factor * factor[column][None, :, :], axis=1)
        pivot = jnp.sqrt(column_values[column])
        keep = (row_ids >= column).astype(source.dtype)[:, None]
        factor = factor.at[:, column, :].set(keep * column_values / pivot[None, :])
    inverse = jnp.zeros_like(source)
    eye_table = jnp.eye(order, dtype=source.dtype)
    for row in range(order):
        row_values = eye_table[row][:, None] - jnp.sum(factor[row][:, None, :] * inverse, axis=0)
        inverse = inverse.at[row].set(row_values / factor[row, row][None, :])
    return (jnp.transpose(factor, (2, 0, 1)), jnp.transpose(inverse, (2, 0, 1)))


def apply_tiles(selector, tile_block, source):
    chosen = jnp.einsum("rp,pkn->rkn", selector, source, preferred_element_type=jnp.float32).astype(
        jnp.bfloat16
    )
    return jnp.einsum("rkj,rji->rki", chosen, tile_block, preferred_element_type=jnp.float32)


def shards(tests, block_inverse, face_weight, mixing, far_tiles, far_column, aggregate, owner_map):
    relaxed = tests
    for sweep_index in range(SWEEPS):
        padded = with_halo(relaxed, (("wide", 0), ("narrow", 3)), 1)
        relaxed = relax_step(relaxed, padded, block_inverse, face_weight, mixing)
    planes = relaxed.shape[0]
    test_count = relaxed.shape[1]
    tile_nodes = relaxed.shape[3] * relaxed.shape[4]
    plane_values = relaxed.astype(jnp.bfloat16).reshape(planes, 3 * test_count, tile_nodes)
    far_local = far_tiles[:, 0]
    slot_count = far_local.shape[1]
    reach_devices = (slot_count - 1) // 2
    plane_ids = jnp.arange(planes, dtype=jnp.int32)
    correction = jnp.zeros((planes, 3 * test_count, tile_nodes), jnp.float32)
    for slot_index in range(slot_count):
        offset = slot_index - reach_devices
        selector = (far_column[:, 0, slot_index][:, None] == plane_ids[None, :]).astype(
            jnp.bfloat16
        )
        tiles_now = far_local[:, slot_index]
        if offset == 0:
            correction = correction + apply_tiles(selector, tiles_now, plane_values)
        else:
            moved_tiles, moved_selector = shifted_2((tiles_now, selector), "wide", offset)
            partial_product = apply_tiles(moved_selector, moved_tiles, plane_values)
            correction = correction + shifted_2(partial_product, "wide", -offset)
    combined = relaxed + correction.reshape(relaxed.shape)
    agg_dev = owner_map.shape[0]
    narrow_count = lax.axis_size("narrow")
    agg_width = agg_dev * narrow_count
    labels = aggregate.reshape(planes, tile_nodes)
    onehots = (labels[:, :, None] == jnp.arange(agg_width, dtype=jnp.int32)[None, None, :]).astype(
        jnp.float32
    )
    vec_planes = combined.reshape(planes, test_count, 3, tile_nodes)

    def gram_step(totals, inputs):
        values, onehot = inputs
        outer_sum = jnp.sum(values[:, None] * values[None, :], axis=2).reshape(
            test_count * test_count, tile_nodes
        )
        return (
            (
                totals[0] + jnp.dot(outer_sum, onehot, precision=highest),
                totals[1] + jnp.sum(onehot, axis=0),
            ),
            None,
        )

    start_totals = (
        jnp.zeros((test_count * test_count, agg_width), jnp.float32),
        jnp.zeros((agg_width,), jnp.float32),
    )
    (gram_part, counts), unused_out = lax.scan(gram_step, start_totals, (vec_planes, onehots))
    gram_home, count_home = (
        lax.psum_scatter(gram_part, "narrow", scatter_dimension=1, tiled=True),
        lax.psum_scatter(counts[None, :], "narrow", scatter_dimension=1, tiled=True),
    )
    eye_k = jnp.eye(test_count, dtype=jnp.float32)
    shifted = (
        gram_home.T.reshape(agg_dev, test_count, test_count) / (3.0 * count_home[0])[:, None, None]
        + ridge_shift * eye_k
    )
    slot_order = jnp.arange(agg_dev, dtype=jnp.int32)
    same_owner = (owner_map[:, None] == owner_map[None, :]) & (
        slot_order[None, :] < slot_order[:, None]
    )
    within = jnp.sum(same_owner.astype(jnp.int32), axis=1)
    target = owner_map * SLOT + within
    device_count = lax.axis_size("wide") * narrow_count
    send_table = (
        jnp.arange(device_count * SLOT, dtype=jnp.int32)[:, None] == target[None, :]
    ).astype(jnp.float32)
    packed = jnp.dot(
        send_table, shifted.reshape(agg_dev, test_count * test_count), precision=highest
    )
    occupied = jnp.sum(send_table, axis=1)
    received, filled = (
        lax.all_to_all(packed, ("wide", "narrow"), split_axis=0, concat_axis=0, tiled=True),
        lax.all_to_all(occupied, ("wide", "narrow"), split_axis=0, concat_axis=0, tiled=True),
    )
    slots_total = received.shape[0]
    padded_mats = (
        received.reshape(slots_total, test_count, test_count)
        + (1.0 - filled)[:, None, None] * eye_k
    )
    lower_factor, inverse = factorize(padded_mats)
    coarse_rows = (
        jnp.swapaxes(lower_factor, 1, 2).reshape(slots_total, test_count * test_count)
        * filled[:, None]
    )
    returned = lax.all_to_all(
        inverse.reshape(slots_total, test_count * test_count),
        ("wide", "narrow"),
        split_axis=0,
        concat_axis=0,
        tiled=True,
    )
    inverse_home = jnp.dot(send_table.T, returned, precision=highest)
    all_inverse = lax.all_gather(inverse_home.T, "narrow", axis=1, tiled=True)

    def project_step(unused_carry, inputs):
        values, onehot = inputs
        lookup = jnp.dot(all_inverse, onehot.T, precision=highest).reshape(
            test_count, test_count, tile_nodes
        )
        return (unused_carry, jnp.sum(lookup[:, :, None, :] * values[None, :, :, :], axis=1))

    unused_final, projected = lax.scan(
        project_step, jnp.zeros((), jnp.float32), (vec_planes, onehots)
    )
    prolong = projected.reshape(relaxed.shape)
    return (prolong, coarse_rows[None])


def solution(mesh):
    in_specs = (
        P("wide", None, None, "narrow", None),
        P("wide", None, None, "narrow", None),
        P("wide", None, "narrow", None),
        P(),
        P("wide", "narrow", None, None, None),
        P("wide", "narrow", None),
        P("wide", "narrow", None),
        P(("wide", "narrow")),
    )
    out_specs = (P("wide", None, None, "narrow", None), P(("wide", "narrow"), None, None))
    return jax.shard_map(shards, mesh=mesh, in_specs=in_specs, out_specs=out_specs, check_vma=False)
```

profile of v0, /device:TPU:1, one launch (start us, length us, event | category | flops | bytes accessed | tf_op | source)
XLA Modules:
  0.0 629.0 jit_solution(16009865726621269655)
XLA Ops:
  25.2 6.1 collective-permute-start.13
  32.5 10.0 %all-to-all-start.1 = ((f32[128,2,1]{1,2,0:T(1,128)}), f32[128,2,1]{1,2,0:T(1,128)S(1)}, u32[]{:S(2)}, u32[]{:S(2)}) async-start(f32[128,2,1]{1,2,0:T(1,128)} %bitcast.88), calls=%async_computation.1 | async-start | bytes 131072 | tf_op jit(solution)/shard_map/all_to_all | solution.py:176
  48.9 8.1 %multiply_add_fusion.47 = (f32[16,32,1,4,64]{4,1,3,2,0:T(8,128)S(1)}, f32[16,32,1,4,64]{4,1,3,2,0:T(8,128)S(1)}, f32[16,32,1,4,64]{4,1,3,2,0:T(8,128)S(1)}) fusion(f32[16,32,3,4,63]{4,1,3,2,0:T(8,128)S(1)} %copy.1844, f32[]{:T(128)} %bitcast.60, f32[]{:T(128)} %bitcast.59, f32[]{:T(128)} %bitcast.58, f32[]{:T(128)} %bitcast.63, f32[]{:T(128)} %bitcast.62, ...), kind=kLoop, calls=%fused_computation.234 | loop fusion | flops 1966080 | bytes 3121188 | tf_op jit(solution)/shard_map/add | solution.py:36
  67.6 6.1 collective-permute-start.3
  73.8 6.2 multiply_add_fusion.62
  79.9 7.8 %multiply_add_fusion.59 = (f32[16,32,1,4,64]{4,1,3,2,0:T(8,128)}, f32[16,32,1,4,64]{4,1,3,2,0:T(8,128)}, f32[16,32,1,4,64]{4,1,3,2,0:T(8,128)}) fusion(f32[17,32,3,4,64]{4,1,3,2,0:T(8,128)S(1)} %get-tuple-element.1078, f32[]{:T(128)} %bitcast.20, f32[]{:T(128)} %bitcast.19, f32[]{:T(128)} %bitcast.18, f32[]{:T(128)} %bitcast.23, f32[]{:T(128)} %bitcast.22, ...), kind=kLoop, calls=%fused_computation.246 | loop fusion | flops 1966080 | bytes 3145764 | tf_op jit(solution)/shard_map/add | solution.py:36
  91.7 6.3 %multiply_add_fusion.53 = (f32[16,32,1,4,64]{4,1,3,2,0:T(8,128)S(1)}, f32[16,32,1,4,64]{4,1,3,2,0:T(8,128)S(1)}, f32[16,32,1,4,64]{4,1,3,2,0:T(8,128)S(1)}, f32[...) fusion(f32[]{:T(128)} %bitcast.40, f32[]{:T(128)} %bitcast.39, ...), kind=kLoop, calls=%fused_computation.240 | loop fusion | flops 2097152 | bytes 6848536 | tf_op jit(solution)/shard_map/add | solution.py:36
  119.9 8.1 %multiply_add_fusion.26 = (f32[16,32,1,4,64]{4,1,3,2,0:T(8,128)S(1)}, f32[16,32,1,4,64]{4,1,3,2,0:T(8,128)S(1)}, f32[16,32,1,4,64]{4,1,3,2,0:T(8,128)S(1)}) fusion(f32[16,32,3,4,63]{4,1,3,2,0:T(8,128)S(1)} %get-tuple-element.1042, f32[]{:T(128)} %bitcast.60, f32[]{:T(128)} %bitcast.59, f32[]{:T(128)} %bitcast.58, f32[]{:T(128)} %bitcast.63, f32[]{:T(128)} %bitcast.62, ...), kind=kLoop, calls=%fused_computation.213 | loop fusion | flops 1966080 | bytes 3121188 | tf_op jit(solution)/shard_map/add | solution.py:36
  135.5 6.5 %collective-permute-start.7 = (f32[18,32,3,1,64]{4,1,3,2,0:T(8,128)}, f32[18,32,3,1,64]{4,1,3,2,0:T(8,128)}, u32[]{:S(2)}, u32[]{:S(2)}) collective-permute-start(f32[18,32,3,1,64]{4,1,3,2,0:T(8,128)} %get-tuple-element.997), channel_id=1, source_target_pairs={{0,1},{2,3},{4,5},{6,7},{8,9},{10,11},{12,13},{14,15},{16,17},{18,... | collective-permute-start | bytes 1327112 | tf_op jit(solution)/shard_map/ppermute | solution.py:22
  186.6 8.1 %multiply_add_fusion.5 = (f32[16,32,1,4,64]{4,1,3,2,0:T(8,128)S(1)}, f32[16,32,1,4,64]{4,1,3,2,0:T(8,128)S(1)}, f32[16,32,1,4,64]{4,1,3,2,0:T(8,128)S(1)}) fusion(f32[16,32,3,4,63]{4,1,3,2,0:T(8,128)S(1)} %get-tuple-element.1017, f32[]{:T(128)} %bitcast.60, f32[]{:T(128)} %bitcast.59, f32[]{:T(128)} %bitcast.58, f32[]{:T(128)} %bitcast.63, f32[]{:T(128)} %bitcast.62, ...), kind=kLoop, calls=%fused_computation.192 | loop fusion | flops 1966080 | bytes 3121188 | tf_op jit(solution)/shard_map/add | solution.py:36
  202.7 6.5 %collective-permute-start.11 = (f32[18,32,3,1,64]{4,1,3,2,0:T(8,128)}, f32[18,32,3,1,64]{4,1,3,2,0:T(8,128)}, u32[]{:S(2)}, u32[]{:S(2)}) collective-permute-start(f32[18,32,3,1,64]{4,1,3,2,0:T(8,128)} %get-tuple-element.995), channel_id=1, source_target_pairs={{0,1},{2,3},{4,5},{6,7},{8,9},{10,11},{12,13},{14,15},{16,17},{18,... | collective-permute-start | bytes 1327112 | tf_op jit(solution)/shard_map/ppermute | solution.py:22
  209.2 6.4 %multiply_add_fusion.17 = (f32[16,32,1,4,64]{4,1,3,2,0:T(8,128)}, f32[16,32,1,4,64]{4,1,3,2,0:T(8,128)S(1)}, f32[16,32,1,4,64]{4,1,3,2,0:T(8,128)S(1)}, f32[16,3...) fusion(f32[]{:T(128)} %bitcast.20, f32[]{:T(128)} %bitcast.19, ...), kind=kLoop, calls=%fused_computation.204 | loop fusion | flops 2097152 | bytes 5963800 | tf_op jit(solution)/shard_map/add | solution.py:36
  224.2 23.4 %collective-permute-done.11 = f32[18,32,3,1,64]{4,1,3,2,0:T(8,128)} collective-permute-done((f32[18,32,3,1,64]{4,1,3,2,0:T(8,128)}, f32[18,32,3,1,64]{4,1,3,2,0:T(8,128)}, u32[]{:S(2)}, u32[]{:S(2)}) %collective-permute-start.11) | collective-permute-done | bytes 442400 | tf_op jit(solution)/shard_map/ppermute | solution.py:22
  257.0 15.0 %collective-permute-done.10 = f32[18,32,3,1,64]{4,1,3,2,0:T(8,128)S(1)} collective-permute-done((f32[18,32,3,1,64]{4,1,3,2,0:T(8,128)S(1)}, f32[18,32,3,1,64]{4,1,3,2,0:T(8,128)S(1)}, u32[]{:S(2)}, u32[]{:S(2)}) %collective-permute-start.10) | collective-permute-done | bytes 442400 | tf_op jit(solution)/shard_map/ppermute | solution.py:23
  306.0 7.4 %collective-permute-done.14 = f32[16,96,256]{2,1,0:T(8,128)} collective-permute-done((f32[16,96,256]{2,1,0:T(8,128)}, f32[16,96,256]{2,1,0:T(8,128)}, u32[]{:S(2)}, u32[]{:S(2)}) %collective-permute-start.14) | collective-permute-done | bytes 1572896 | tf_op jit(solution)/shard_map/ppermute | solution.py:30
  313.4 6.4 %collective-permute-done.17 = f32[16,96,256]{2,1,0:T(8,128)} collective-permute-done((f32[16,96,256]{2,1,0:T(8,128)}, f32[16,96,256]{2,1,0:T(8,128)}, u32[]{:S(2)}, u32[]{:S(2)}) %collective-permute-start.17) | collective-permute-done | bytes 1572896 | tf_op jit(solution)/shard_map/ppermute | solution.py:30
  340.3 54.2 %while.88 = (s32[]{:T(128)}, f32[1024,128]{1,0:T(8,128)S(1)}, f32[128]{0:T(128)S(1)}, f32[16,32,3,256]{3,1,2,0:T(8,128)S(1)}, f32[16,256,128]{2,1,0:T(8,128)}, /*index=5*/s32[]{:T(128)}, s32[]{:T(128)}) while((s32[]{:T(128)}, f32[1024,128]{1,0:T(8,128)S(1)}, f32[128]{0:T(128)S(1)}, f32[16,32,3,256]{3,1,2,0:T(8,128)S(1)}, ...), condition=%wide.region_4.5_spmd.clone, body=%wide.region_1.4_spmd.clone.sunk | while | flops 404258944 | bytes 4000352 | solution.py:150
  396.7 16.2 %reduce-scatter.9.cloned.1.call-done = f32[64,1]{1,0:T(8,128)} async-done(((f32[128,1]{1,0:T(8,128)}), f32[64,1]{1,0:T(8,128)}) %reduce-scatter.9.cloned.1.call-update) | async-done | bytes 272
  413.7 20.5 %reduce-scatter.7.cloned.1.call-done = f32[64,1024]{1,0:T(8,128)} async-done(((f32[128,1024]{1,0:T(8,128)}), f32[64,1024]{1,0:T(8,128)}) %reduce-scatter.7.cloned.1.call-update) | async-done | bytes 262160
  437.6 7.5 %all-to-all-start = ((f32[128,2,1024]{2,1,0:T(2,128)}), f32[128,2,1024]{2,1,0:T(2,128)S(1)}, u32[]{:S(2)}, u32[]{:S(2)}) async-start(f32[128,2,1024]{2,1,0:T(2,128)} %copy.1501), calls=%async_computation | async-start | bytes 2097152 | tf_op jit(solution)/shard_map/all_to_all | solution.py:175
  446.6 17.8 %all-to-all-done = f32[128,2,1024]{2,1,0:T(2,128)S(1)} async-done(((f32[128,2,1024]{2,1,0:T(2,128)}), f32[128,2,1024]{2,1,0:T(2,128)S(1)}, u32[]{:S(2)}, u32[]{:S(2)}) %all-to-all-start) | async-done | bytes 1048608 | tf_op jit(solution)/shard_map/all_to_all | solution.py:175
  516.8 17.9 %all-to-all-done.2 = f32[128,2,1024]{2,1,0:T(2,128)S(1)} async-done(((f32[128,2,1024]{2,1,0:T(2,128)}), f32[128,2,1024]{2,1,0:T(2,128)S(1)}, u32[]{:S(2)}, u32[]{:S(2)}) %all-to-all-start.2) | async-done | bytes 1048608 | tf_op jit(solution)/shard_map/all_to_all | solution.py:188
  536.0 10.1 %all_gather.3 = f32[1024,128]{0,1:T(8,128)S(1)} all-gather(f32[1024,64]{0,1:T(8,128)S(1)} %fusion.38), channel_id=1, replica_groups=mesh['wide'=64,'narrow'=2] {'narrow'}, dimensions={1}, use_global_device_ids=true | all-gather | bytes 786432 | tf_op jit(solution)/shard_map/all_gather | solution.py:196
  546.3 70.6 %while.87 = (s32[]{:T(128)}, f32[16,32,3,256]{3,2,1,0:T(4,128)}, f32[16,256,128]{2,1,0:T(8,128)}, f32[1024,128]{1,0:T(8,128)S(1)}, f32[16,32,3,256]{3,1,2,0:T(8,128)}, /*index=5*/s32[]{:T(128)}) while((s32[]{:T(128)}, f32[16,32,3,256]{3,2,1,0:T(4,128)}, f32[16,256,128]{2,1,0:T(8,128)}, f32[1024,128]{1,0:T(8,128)S(1)}, ...), condition=%wide.region_73.74_spmd, body=%wide.region_71.73_spmd.sunk | while | flops 404201472 | bytes 5473353 | solution.py:205
  (778 shorter events, 381.3 us)
Async XLA Ops:
  8.9 54.2 %collective-permute-start.1 = (f32[1,32,3,4,64]{4,1,3,2,0:T(8,128)}, f32[1,32,3,4,64]{4,1,3,2,0:T(8,128)}, u32[]{:S(2)}, u32[]{:S(2)}) collective-permute-start(f32[1,32,3,4,64]{4,1,3,2,0:T(8,128)} %copy.1842), channel_id=1, source_target_pairs={{0,2},{2,4},{4,6},{6,8},{8,10},{10,12},{12,14},{14,16},{16,18},{18... | collective-permute-start | bytes 294920 | tf_op jit(solution)/shard_map/ppermute | solution.py:22
  14.2 51.0 %collective-permute-start = (f32[1,32,3,4,64]{4,1,3,2,0:T(8,128)}, f32[1,32,3,4,64]{4,1,3,2,0:T(8,128)}, u32[]{:S(2)}, u32[]{:S(2)}) collective-permute-start(f32[1,32,3,4,64]{4,1,3,2,0:T(8,128)} %copy.1841), channel_id=1, source_target_pairs={{2,0},{4,2},{6,4},{8,6},{10,8},{12,10},{14,12},{16,14},{18,16},{20... | collective-permute-start | bytes 294920 | tf_op jit(solution)/shard_map/ppermute | solution.py:23
  16.9 272.5 %collective-permute-start.12 = (bf16[16,16]{1,0:T(8,128)(2,1)S(1)}, bf16[16,16]{1,0:T(8,128)(2,1)S(1)}, u32[]{:S(2)}, u32[]{:S(2)}) collective-permute-start(bf16[16,16]{1,0:T(8,128)(2,1)S(1)} %fusion.201), channel_id=1, source_target_pairs={{0,126},{2,0},{4,2},{6,4},{8,6},{10,8},{12,10},{14,12},{16,14},{18... | collective-permute-start | bytes 1544 | tf_op jit(solution)/shard_map/ppermute | solution.py:30
  25.2 267.2 %collective-permute-start.13 = (bf16[16,256,256]{2,1,0:T(8,128)(2,1)}, bf16[16,256,256]{2,1,0:T(8,128)(2,1)}, u32[]{:S(2)}, u32[]{:S(2)}) collective-permute-start(bf16[16,256,256]{2,1,0:T(8,128)(2,1)} %get-tuple-element.993), channel_id=1, source_target_pairs={{0,126},{2,0},{4,2},{6,4},{8,6},{10,8},{12,10},{14,12},{16,14},{18... | collective-permute-start | bytes 6291464 | tf_op jit(solution)/shard_map/ppermute | solution.py:30
  31.4 259.5 %collective-permute-start.15 = (bf16[16,16]{1,0:T(8,128)(2,1)S(1)}, bf16[16,16]{1,0:T(8,128)(2,1)S(1)}, u32[]{:S(2)}, u32[]{:S(2)}) collective-permute-start(bf16[16,16]{1,0:T(8,128)(2,1)S(1)} %fusion.204), channel_id=1, source_target_pairs={{0,2},{2,4},{4,6},{6,8},{8,10},{10,12},{12,14},{14,16},{16,18},{18... | collective-permute-start | bytes 1544 | tf_op jit(solution)/shard_map/ppermute | solution.py:30
  32.5 405.1 %all-to-all-start.1 = ((f32[128,2,1]{1,2,0:T(1,128)}), f32[128,2,1]{1,2,0:T(1,128)S(1)}, u32[]{:S(2)}, u32[]{:S(2)}) async-start(f32[128,2,1]{1,2,0:T(1,128)} %bitcast.88), calls=%async_computation.1 | async-start | bytes 131072 | tf_op jit(solution)/shard_map/all_to_all | solution.py:176
  42.5 370.4 %reduce-scatter.9.cloned.1.call-start = ((), (), s32[]{:S(2)}) async-start(), calls=%async_computation.6 | async-start | bytes 98304
  66.3 23.5 %collective-permute-start.2 = (f32[18,32,3,1,64]{4,1,3,2,0:T(8,128)S(1)}, f32[18,32,3,1,64]{4,1,3,2,0:T(8,128)S(1)}, u32[]{:S(2)}, u32[]{:S(2)}) collective-permute-start(f32[18,32,3,1,64]{4,1,3,2,0:T(8,128)S(1)} %get-tuple-element.1004), channel_id=1, source_target_pairs={{1,0},{3,2},{5,4},{7,6},{9,8},{11,10},{13,12},{15,14},{17,16},{19,... | collective-permute-start | bytes 1327112 | tf_op jit(solution)/shard_map/ppermute | solution.py:23
  67.6 23.1 %collective-permute-start.3 = (f32[18,32,3,1,64]{4,1,3,2,0:T(8,128)S(1)}, f32[18,32,3,1,64]{4,1,3,2,0:T(8,128)S(1)}, u32[]{:S(2)}, u32[]{:S(2)}) collective-permute-start(f32[18,32,3,1,64]{4,1,3,2,0:T(8,128)S(1)} %get-tuple-element.1003), channel_id=1, source_target_pairs={{0,1},{2,3},{4,5},{6,7},{8,9},{10,11},{12,13},{14,15},{16,17},{18,... | collective-permute-start | bytes 1327112 | tf_op jit(solution)/shard_map/ppermute | solution.py:22
  110.2 171.9 %copy-start.1 = (f32[16,32,1,4,64]{4,1,3,2,0:T(8,128)}, f32[16,32,1,4,64]{4,1,3,2,0:T(8,128)S(1)}, u32[]{:S(2)}) copy-start(f32[16,32,1,4,64]{4,1,3,2,0:T(8,128)S(1)} %get-tuple-element.1061) | copy-start | bytes 1572868
  112.5 21.6 %collective-permute-start.4 = (f32[1,32,3,4,64]{4,1,3,2,0:T(8,128)S(1)}, f32[1,32,3,4,64]{4,1,3,2,0:T(8,128)S(1)}, u32[]{:S(2)}, u32[]{:S(2)}) collective-permute-start(f32[1,32,3,4,64]{4,1,3,2,0:T(8,128)S(1)} %get-tuple-element.1058), channel_id=1, source_target_pairs={{2,0},{4,2},{6,4},{8,6},{10,8},{12,10},{14,12},{16,14},{18,16},{20... | collective-permute-start | bytes 294920 | tf_op jit(solution)/shard_map/ppermute | solution.py:23
  116.7 17.4 %collective-permute-start.5 = (f32[1,32,3,4,64]{4,1,3,2,0:T(8,128)S(1)}, f32[1,32,3,4,64]{4,1,3,2,0:T(8,128)S(1)}, u32[]{:S(2)}, u32[]{:S(2)}) collective-permute-start(f32[1,32,3,4,64]{4,1,3,2,0:T(8,128)S(1)} %get-tuple-element.1057), channel_id=1, source_target_pairs={{0,2},{2,4},{4,6},{6,8},{8,10},{10,12},{12,14},{14,16},{16,18},{18... | collective-permute-start | bytes 294920 | tf_op jit(solution)/shard_map/ppermute | solution.py:22
  135.5 25.1 %collective-permute-start.7 = (f32[18,32,3,1,64]{4,1,3,2,0:T(8,128)}, f32[18,32,3,1,64]{4,1,3,2,0:T(8,128)}, u32[]{:S(2)}, u32[]{:S(2)}) collective-permute-start(f32[18,32,3,1,64]{4,1,3,2,0:T(8,128)} %get-tuple-element.997), channel_id=1, source_target_pairs={{0,1},{2,3},{4,5},{6,7},{8,9},{10,11},{12,13},{14,15},{16,17},{18,... | collective-permute-start | bytes 1327112 | tf_op jit(solution)/shard_map/ppermute | solution.py:22
  142.0 26.5 %collective-permute-start.6 = (f32[18,32,3,1,64]{4,1,3,2,0:T(8,128)}, f32[18,32,3,1,64]{4,1,3,2,0:T(8,128)S(1)}, u32[]{:S(2)}, u32[]{:S(2)}) collective-permute-start(f32[18,32,3,1,64]{4,1,3,2,0:T(8,128)} %get-tuple-element.998), channel_id=1, source_target_pairs={{1,0},{3,2},{5,4},{7,6},{9,8},{11,10},{13,12},{15,14},{17,16},{19,... | collective-permute-start | bytes 1327112 | tf_op jit(solution)/shard_map/ppermute | solution.py:23
  181.0 19.8 %collective-permute-start.8 = (f32[1,32,3,4,64]{4,1,3,2,0:T(8,128)S(1)}, f32[1,32,3,4,64]{4,1,3,2,0:T(8,128)S(1)}, u32[]{:S(2)}, u32[]{:S(2)}) collective-permute-start(f32[1,32,3,4,64]{4,1,3,2,0:T(8,128)S(1)} %get-tuple-element.1033), channel_id=1, source_target_pairs={{2,0},{4,2},{6,4},{8,6},{10,8},{12,10},{14,12},{16,14},{18,16},{20... | collective-permute-start | bytes 294920 | tf_op jit(solution)/shard_map/ppermute | solution.py:23
  183.0 18.2 %collective-permute-start.9 = (f32[1,32,3,4,64]{4,1,3,2,0:T(8,128)S(1)}, f32[1,32,3,4,64]{4,1,3,2,0:T(8,128)S(1)}, u32[]{:S(2)}, u32[]{:S(2)}) collective-permute-start(f32[1,32,3,4,64]{4,1,3,2,0:T(8,128)S(1)} %get-tuple-element.1032), channel_id=1, source_target_pairs={{0,2},{2,4},{4,6},{6,8},{8,10},{10,12},{12,14},{14,16},{16,18},{18... | collective-permute-start | bytes 294920 | tf_op jit(solution)/shard_map/ppermute | solution.py:22
  200.8 94.9 %collective-permute-start.16 = (bf16[16,256,256]{2,1,0:T(8,128)(2,1)}, bf16[16,256,256]{2,1,0:T(8,128)(2,1)}, u32[]{:S(2)}, u32[]{:S(2)}) collective-permute-start(bf16[16,256,256]{2,1,0:T(8,128)(2,1)} %get-tuple-element.994), channel_id=1, source_target_pairs={{0,2},{2,4},{4,6},{6,8},{8,10},{10,12},{12,14},{14,16},{16,18},{18... | collective-permute-start | bytes 6291464 | tf_op jit(solution)/shard_map/ppermute | solution.py:30
  202.7 44.9 %collective-permute-start.11 = (f32[18,32,3,1,64]{4,1,3,2,0:T(8,128)}, f32[18,32,3,1,64]{4,1,3,2,0:T(8,128)}, u32[]{:S(2)}, u32[]{:S(2)}) collective-permute-start(f32[18,32,3,1,64]{4,1,3,2,0:T(8,128)} %get-tuple-element.995), channel_id=1, source_target_pairs={{0,1},{2,3},{4,5},{6,7},{8,9},{10,11},{12,13},{14,15},{16,17},{18,... | collective-permute-start | bytes 1327112 | tf_op jit(solution)/shard_map/ppermute | solution.py:22
  247.6 24.4 %collective-permute-start.10 = (f32[18,32,3,1,64]{4,1,3,2,0:T(8,128)S(1)}, f32[18,32,3,1,64]{4,1,3,2,0:T(8,128)S(1)}, u32[]{:S(2)}, u32[]{:S(2)}) collective-permute-start(f32[18,32,3,1,64]{4,1,3,2,0:T(8,128)S(1)} %copy-done.20), channel_id=1, source_target_pairs={{1,0},{3,2},{5,4},{7,6},{9,8},{11,10},{13,12},{15,14},{17,16},{19,... | collective-permute-start | bytes 1327112 | tf_op jit(solution)/shard_map/ppermute | solution.py:23
  295.7 17.7 %collective-permute-start.14 = (f32[16,96,256]{2,1,0:T(8,128)}, f32[16,96,256]{2,1,0:T(8,128)}, u32[]{:S(2)}, u32[]{:S(2)}) collective-permute-start(f32[16,96,256]{2,1,0:T(8,128)} %fusion.29), channel_id=1, source_target_pairs={{0,2},{2,4},{4,6},{6,8},{8,10},{10,12},{12,14},{14,16},{16,18},{18... | collective-permute-start | bytes 4718600 | tf_op jit(solution)/shard_map/ppermute | solution.py:30
  298.9 20.8 %collective-permute-start.17 = (f32[16,96,256]{2,1,0:T(8,128)}, f32[16,96,256]{2,1,0:T(8,128)}, u32[]{:S(2)}, u32[]{:S(2)}) collective-permute-start(f32[16,96,256]{2,1,0:T(8,128)} %fusion.26), channel_id=1, source_target_pairs={{0,126},{2,0},{4,2},{6,4},{8,6},{10,8},{12,10},{14,12},{16,14},{18... | collective-permute-start | bytes 4718600 | tf_op jit(solution)/shard_map/ppermute | solution.py:30
  395.4 38.8 %reduce-scatter.7.cloned.1.call-start = ((), (), s32[]{:S(2)}) async-start(), calls=%async_computation.5 | async-start | bytes 786432
  437.6 26.8 %all-to-all-start = ((f32[128,2,1024]{2,1,0:T(2,128)}), f32[128,2,1024]{2,1,0:T(2,128)S(1)}, u32[]{:S(2)}, u32[]{:S(2)}) async-start(f32[128,2,1024]{2,1,0:T(2,128)} %copy.1501), calls=%async_computation | async-start | bytes 2097152 | tf_op jit(solution)/shard_map/all_to_all | solution.py:175
  511.2 23.6 %all-to-all-start.2 = ((f32[128,2,1024]{2,1,0:T(2,128)}), f32[128,2,1024]{2,1,0:T(2,128)S(1)}, u32[]{:S(2)}, u32[]{:S(2)}) async-start(f32[128,2,1024]{2,1,0:T(2,128)} %all_to_all.24), calls=%async_computation.2 | async-start | bytes 2097152 | tf_op jit(solution)/shard_map/all_to_all | solution.py:188
  (25 other events, 798.8 us)
Sparse Core Ops, SparseCore 0:
  395.6 17.2 reduce-scatter.8
  415.8 18.3 reduce-scatter.6
where the time goes:
time: 640 us; the launch traced here: 629 us
  other arithmetic  205 us (32%)
  waiting for transfers between devices  131 us (20%)
  local copies, waits for them, and re-layouts  113 us (18%)
  matrix products  78 us (12%)
  starting transfers between devices  72.7 us (11%)
  between operations  18 us (3%)
  blocking collectives  10.1 us (2%)
    add x25, other arithmetic, mix_components(): matrix[component, 0] * field_values[:, :, 0]  129 us
    unnamed x4, waiting for transfers between devices  36.7 us
    dot_general x16, matrix products, gram_step(): jnp.dot(outer_sum, onehot, precision=highest)  32.4 us
    ppermute x6, starting transfers between devices, with_halo(): before = lax.ppermute(last, axis, up)  30.5 us
    dot_general x16, matrix products, project_step(): jnp.dot(all_inverse, onehot.T, precision=highest)  30.3 us
    ppermute x6, waiting for transfers between devices, with_halo(): before = lax.ppermute(last, axis, up)  27.9 us
    unnamed x187, local copies, waits for them, and re-layouts  23.5 us
    all_to_all x1, waiting for transfers between devices, shards(): lax.all_to_all(inverse.reshape(slots_total, test_count * test_count), ('w...  17.9 us
  transfers between devices with their start and end apart: 23, of which 11 were waited for; matrix products, arithmetic and copies ran while one was open for 43% of the time, Pallas kernels for 0%

commit v1 on v0

v1 whole, which is shorter than its diff:
```python
import functools

import jax
import jax.numpy as jnp
from jax import lax
from jax.experimental import pallas as pl
from jax.experimental.pallas import tpu as pltpu
from jax.sharding import PartitionSpec as P

MESH = pl.DeviceIdType.MESH
SWEEPS = 3
SLOT = 2
K = 32
ROWS = 3 * K
PLANES = 16
NODES = 256
WIDTH = 128
RIDGE = 0.001

BLOCKS = [(k, b) for k in range(K) for b in range(k // 8, K // 8)]
TRI = 8 * len(BLOCKS)
STARTS = {}
for place, (block_k, block_b) in enumerate(BLOCKS):
    STARTS.setdefault(block_k, 8 * place)
GRAM_ROWS = TRI + 16


def split3(x):
    hi = x.astype(jnp.bfloat16)
    rest = x - hi.astype(jnp.float32)
    mid = rest.astype(jnp.bfloat16)
    low = (rest - mid.astype(jnp.float32)).astype(jnp.bfloat16)
    return hi, mid, low


def relax_kernel(
    n_wide,
    tests_hbm, bi_ref, fw_ref, mix_ref, tiles_hbm, col_ref, label_ref,
    comb_ref, gram_ref,
    x0, x1, x2, coef, ysend, yrecv, ydup, from_left, planes, from_right, tiles, outer, acc, gram_in,
    local_sems, xsend_sems, xrecv_sems, ysend_sems, yrecv_sems, psend_sems, precv_sems, gsend_sem, grecv_sem,
):
    w = lax.axis_index("wide")
    n = lax.axis_index("narrow")
    right = lax.rem(w + 1, n_wide)
    left = lax.rem(w + n_wide - 1, n_wide)
    other = 1 - n
    fields = [x0, x1, x2]

    tests_copy = pltpu.make_async_copy(tests_hbm, x0.at[pl.ds(1, PLANES)], local_sems.at[0])
    tests_copy.start()
    tiles_copy = pltpu.make_async_copy(tiles_hbm, tiles, local_sems.at[1])
    tiles_copy.start()

    barrier = pltpu.get_barrier_semaphore()
    for target in ((left, n), (right, n), (w, other)):
        pl.semaphore_signal(barrier, inc=1, device_id=target, device_id_type=MESH)
    pl.semaphore_wait(barrier, 3)

    lane = lax.broadcasted_iota(jnp.int32, (K + 16, WIDTH), 1)
    low_half = lane < 64
    is_low = n == 0

    def pack_row(first, second):
        chosen = jnp.where(is_low, second, first)
        turned = pltpu.roll(chosen, 64, 1)
        a = jnp.where(is_low, turned, chosen)[0:48]
        b = jnp.where(is_low, chosen, turned)[48:96]
        return jnp.where(low_half, a, b).astype(jnp.bfloat16)

    def y_copy(s):
        return pltpu.make_async_remote_copy(
            src_ref=ysend.at[s], dst_ref=yrecv.at[s], send_sem=ysend_sems.at[s], recv_sem=yrecv_sems.at[s],
            device_id=(w, other), device_id_type=MESH,
        )

    def x_copies(s):
        up = pltpu.make_async_remote_copy(
            src_ref=fields[s].at[PLANES], dst_ref=fields[s].at[0], send_sem=xsend_sems.at[2 * s],
            recv_sem=xrecv_sems.at[2 * s], device_id=(right, n), device_id_type=MESH,
        )
        down = pltpu.make_async_remote_copy(
            src_ref=fields[s].at[1], dst_ref=fields[s].at[PLANES + 1], send_sem=xsend_sems.at[2 * s + 1],
            recv_sem=xrecv_sems.at[2 * s + 1], device_id=(left, n), device_id_type=MESH,
        )
        return up, down

    tests_copy.wait()

    def pack_tests(p, carry):
        ysend[0, p] = pack_row(x0[p + 1, :, 0:128], x0[p + 1, :, 128:256])
        return carry

    for copy in x_copies(0):
        copy.start()
    lax.fori_loop(0, PLANES, pack_tests, 0)
    y_copy(0).start()

    lane_wide = lax.broadcasted_iota(jnp.int32, (8, NODES), 1)
    z_place = lax.rem(lane_wide, 64)

    def make_coef(p, carry):
        inv_rows = [jnp.broadcast_to(bi_ref[p, i : i + 1, :], (8, NODES)) for i in range(9)]
        edges = [
            jnp.logical_and(p == PLANES - 1, w == n_wide - 1),
            jnp.logical_and(p == 0, w == 0),
            jnp.logical_and(lane_wide >= 192, n == 1),
            jnp.logical_and(lane_wide < 64, n == 0),
            z_place == 63,
            z_place == 0,
        ]
        for d in range(6):
            weight = 0.5 * jnp.broadcast_to(fw_ref[p, d : d + 1, :], (8, NODES))
            weight = jnp.where(edges[d], 0.0, weight)
            for a in range(3):
                for b in range(3):
                    total = inv_rows[3 * a] * mix_ref[9 * d + b]
                    total += inv_rows[3 * a + 1] * mix_ref[9 * d + 3 + b]
                    total += inv_rows[3 * a + 2] * mix_ref[9 * d + 6 + b]
                    coef[p, 9 * d + 3 * a + b] = total * weight
        return carry

    lax.fori_loop(0, PLANES, make_coef, 0)

    low8 = low_half[0:8]

    def sweep_plane(s, p):
        src = fields[s]
        packed = yrecv[s, p].astype(jnp.float32)
        turned = pltpu.roll(packed, 64, 1)
        ydup[0:48] = jnp.where(low_half, packed, turned)
        ydup[48:96] = jnp.where(low_half, turned, packed)
        for kb in range(K // 8):
            near = []
            own = []
            for c in range(3):
                rows = pl.ds(c * K + kb * 8, 8)
                mid = src[p + 1, rows, :]
                own.append(mid)
                c0, c1 = mid[:, 0:128], mid[:, 128:256]
                r0, r1 = pltpu.roll(c0, 64, 1), pltpu.roll(c1, 64, 1)
                dup = ydup[rows]
                between = jnp.where(low8, r0, r1)
                y_up = jnp.concatenate([between, jnp.where(low8, r1, dup)], axis=1)
                y_down = jnp.concatenate([jnp.where(low8, dup, r0), between], axis=1)
                z_up = jnp.concatenate([pltpu.roll(c0, 127, 1), pltpu.roll(c1, 127, 1)], axis=1)
                z_down = jnp.concatenate([pltpu.roll(c0, 1, 1), pltpu.roll(c1, 1, 1)], axis=1)
                near.append([src[p + 2, rows, :], src[p, rows, :], y_up, y_down, z_up, z_down])
            for a in range(3):
                total = 0.5 * own[a]
                for d in range(6):
                    for b in range(3):
                        total += coef[p, 9 * d + 3 * a + b] * near[b][d]
                rows = pl.ds(a * K + kb * 8, 8)
                if s + 1 < SWEEPS:
                    fields[s + 1][p + 1, rows, :] = total
                else:
                    comb_ref[p, rows, :] = total

    def wait_sweep(s):
        for copy in x_copies(s):
            copy.wait()
        y_copy(s).wait()

    for s in range(SWEEPS - 1):
        wait_sweep(s)

        def one_plane(p, carry, s=s):
            sweep_plane(s, p)
            ysend[s + 1, p] = pack_row(fields[s + 1][p + 1, :, 0:128], fields[s + 1][p + 1, :, 128:256])
            return carry

        lax.fori_loop(0, PLANES, one_plane, 0)
        for copy in x_copies(s + 1):
            copy.start()
        y_copy(s + 1).start()

    wait_sweep(SWEEPS - 1)
    chunk_planes = 4
    chunks = PLANES // chunk_planes

    def plane_copies(q):
        span = pl.ds(q * chunk_planes, chunk_planes)
        up = pltpu.make_async_remote_copy(
            src_ref=planes.at[span], dst_ref=from_left.at[span], send_sem=psend_sems.at[2 * q],
            recv_sem=precv_sems.at[2 * q], device_id=(right, n), device_id_type=MESH,
        )
        down = pltpu.make_async_remote_copy(
            src_ref=planes.at[span], dst_ref=from_right.at[span], send_sem=psend_sems.at[2 * q + 1],
            recv_sem=precv_sems.at[2 * q + 1], device_id=(left, n), device_id_type=MESH,
        )
        return up, down

    for q in range(chunks):

        def last_plane(p, carry):
            sweep_plane(SWEEPS - 1, p)
            planes[p] = comb_ref[p].astype(jnp.bfloat16)
            return carry

        lax.fori_loop(q * chunk_planes, (q + 1) * chunk_planes, last_plane, 0)
        for copy in plane_copies(q):
            copy.start()

    tiles_copy.wait()

    acc[...] = jnp.zeros_like(acc)
    ones = jnp.ones((16, NODES), jnp.bfloat16)
    outer[0, TRI:GRAM_ROWS] = ones
    outer[1, TRI:GRAM_ROWS] = jnp.zeros_like(ones)
    outer[2, TRI:GRAM_ROWS] = jnp.zeros_like(ones)

    sources = [from_left, planes, from_right]

    def far_product(r, slot):
        return jnp.dot(
            sources[slot][col_ref[r, slot]], tiles[r, slot], preferred_element_type=jnp.float32
        )

    def near_far(r, carry):
        comb_ref[r] = comb_ref[r] + far_product(r, 1)
        return carry

    lax.fori_loop(0, PLANES, near_far, 0)

    for q in range(chunks):
        for copy in plane_copies(q):
            copy.wait()

    groups = lax.broadcasted_iota(jnp.int32, (WIDTH, NODES), 0)

    def gram_plane(r, carry):
        comb_ref[r] = comb_ref[r] + (far_product(r, 0) + far_product(r, 2))
        member = jnp.where(groups == label_ref[r], 1.0, 0.0).astype(jnp.bfloat16)
        for pair in range(len(BLOCKS) // 2):
            parts = []
            for k, b in BLOCKS[2 * pair : 2 * pair + 2]:
                value = None
                for c in range(3):
                    term = comb_ref[r, c * K + k : c * K + k + 1, :] * comb_ref[r, pl.ds(c * K + 8 * b, 8), :]
                    value = term if value is None else value + term
                parts.append(value)
            pieces = split3(jnp.concatenate(parts, axis=0))
            for i in range(3):
                outer[i, pl.ds(16 * pair, 16), :] = pieces[i]
        total = None
        for i in range(3):
            term = lax.dot_general(
                outer[i], member, (((1,), (1,)), ((), ())), preferred_element_type=jnp.float32
            )
            total = term if total is None else total + term
        acc[...] += total
        return carry

    lax.fori_loop(0, PLANES, gram_plane, 0)

    gram_copy = pltpu.make_async_remote_copy(
        src_ref=acc, dst_ref=gram_in, send_sem=gsend_sem.at[0], recv_sem=grecv_sem.at[0],
        device_id=(w, other), device_id_type=MESH,
    )
    gram_copy.start()
    gram_copy.wait()
    gram_ref[...] = acc[...] + gram_in[...]


def factor_kernel(gram_ref, table_ref, packed_ref, inverse_ref, lower, inv):
    scale = 1.0 / (3.0 * gram_ref[TRI : TRI + 1, :])
    row = lax.broadcasted_iota(jnp.int32, (K, WIDTH), 0)
    columns = []
    for k in range(K):
        first = 8 * (k // 8)
        height = K - first
        column = gram_ref[pl.ds(STARTS[k], height), :] * scale
        columns.append(column + jnp.where(row[first:] == k, RIDGE, 0.0))
    reciprocals = []
    for k in range(K):
        first = 8 * (k // 8)
        at = k - first
        pivot = jnp.sqrt(columns[k][at : at + 1])
        reciprocal = 1.0 / pivot
        reciprocals.append(reciprocal)
        column = jnp.where(row[first:] >= k, columns[k] * reciprocal, 0.0)
        columns[k] = column
        for m in range(k + 1, K):
            begin = 8 * (m // 8)
            columns[m] = columns[m] - column[m - first : m - first + 1] * column[begin - first :]
        lower[pl.ds(K * k, K), :] = (
            column if first == 0 else jnp.concatenate([jnp.zeros((first, WIDTH), jnp.float32), column], axis=0)
        )
    for l in range(K):
        first = 8 * (l // 8)
        solved = jnp.where(row[first:] == l, 1.0, 0.0)
        for m in range(l, K):
            base = 8 * (m // 8)
            value = solved[m - first : m - first + 1] * reciprocals[m]
            here = solved[base - first :]
            here = jnp.where(row[base:] == m, value, jnp.where(row[base:] > m, here - columns[m] * value, here))
            solved = here if base == first else jnp.concatenate([solved[: base - first], here], axis=0)
        inv[pl.ds(STARTS[l], K - first), :] = solved
    for i, piece in enumerate(split3(inv[...])):
        inverse_ref[:, i * WIDTH : (i + 1) * WIDTH] = piece
    table = table_ref[...]
    total = None
    for piece in split3(lower[...]):
        term = lax.dot_general(table, piece, (((1,), (1,)), ((), ())), preferred_element_type=jnp.float32)
        total = term if total is None else total + term
    packed_ref[...] = total


def project_kernel(comb_ref, label_ref, inverse_ref, out_ref, look):
    groups = lax.broadcasted_iota(jnp.int32, (WIDTH, NODES), 0)
    member = jnp.where(groups == label_ref[0], 1.0, 0.0).astype(jnp.bfloat16)
    look[...] = jnp.dot(
        inverse_ref[...], jnp.concatenate([member, member, member], axis=0), preferred_element_type=jnp.float32
    )
    for b in range(K // 8):
        totals = [None] * 3
        for l in range(8 * (b + 1)):
            weight = look[pl.ds(STARTS[l] + 8 * (b - l // 8), 8), :]
            for c in range(3):
                term = weight * comb_ref[0, c * K + l : c * K + l + 1, :]
                totals[c] = term if totals[c] is None else totals[c] + term
        for c in range(3):
            out_ref[0, pl.ds(c * K + 8 * b, 8), :] = totals[c]


def vmem(shape, dtype=jnp.float32):
    return pltpu.VMEM(shape, dtype)


def shards(n_wide, n_narrow, tests, block_inverse, face_weight, mixing, far_tiles, far_column, aggregate, owner_map):
    bf16 = jnp.bfloat16
    whole = pl.BlockSpec(memory_space=pltpu.VMEM)
    any_spec = pl.BlockSpec(memory_space=pl.ANY)
    smem = pl.BlockSpec(memory_space=pltpu.SMEM)
    field = tests.reshape(PLANES, K, 3, NODES).transpose(0, 2, 1, 3).reshape(PLANES, ROWS, NODES)
    labels = aggregate.reshape(PLANES, 1, NODES)

    agg_dev = owner_map.shape[0]
    slot_order = jnp.arange(agg_dev, dtype=jnp.int32)
    same_owner = (owner_map[:, None] == owner_map[None, :]) & (slot_order[None, :] < slot_order[:, None])
    within = jnp.sum(same_owner.astype(jnp.int32), axis=1)
    target = owner_map * SLOT + within
    slots_total = n_wide * n_narrow * SLOT
    own_lane = jnp.arange(WIDTH, dtype=jnp.int32) // agg_dev == lax.axis_index("narrow")
    target_lane = jnp.where(own_lane, jnp.tile(target, n_narrow), -1)
    table = (jnp.arange(slots_total, dtype=jnp.int32)[:, None] == target_lane[None, :]).astype(bf16)

    combined, gram = pl.pallas_call(
        functools.partial(relax_kernel, n_wide),
        out_shape=(
            jax.ShapeDtypeStruct((PLANES, ROWS, NODES), jnp.float32),
            jax.ShapeDtypeStruct((GRAM_ROWS, WIDTH), jnp.float32),
        ),
        in_specs=[any_spec, whole, whole, smem, any_spec, smem, whole],
        out_specs=(whole, whole),
        scratch_shapes=[
            vmem((PLANES + 2, ROWS, NODES)),
            vmem((PLANES + 2, ROWS, NODES)),
            vmem((PLANES + 2, ROWS, NODES)),
            vmem((PLANES, 54, 8, NODES)),
            vmem((SWEEPS, PLANES, 48, WIDTH), bf16),
            vmem((SWEEPS, PLANES, 48, WIDTH), bf16),
            vmem((ROWS, WIDTH)),
            vmem((PLANES, ROWS, NODES), bf16),
            vmem((PLANES, ROWS, NODES), bf16),
            vmem((PLANES, ROWS, NODES), bf16),
            vmem((PLANES, 3, NODES, NODES), bf16),
            vmem((3, GRAM_ROWS, NODES), bf16),
            vmem((GRAM_ROWS, WIDTH)),
            vmem((GRAM_ROWS, WIDTH)),
            pltpu.SemaphoreType.DMA((2,)),
            pltpu.SemaphoreType.DMA((2 * SWEEPS,)),
            pltpu.SemaphoreType.DMA((2 * SWEEPS,)),
            pltpu.SemaphoreType.DMA((SWEEPS,)),
            pltpu.SemaphoreType.DMA((SWEEPS,)),
            pltpu.SemaphoreType.DMA((8,)),
            pltpu.SemaphoreType.DMA((8,)),
            pltpu.SemaphoreType.DMA((1,)),
            pltpu.SemaphoreType.DMA((1,)),
        ],
        compiler_params=pltpu.CompilerParams(
            collective_id=0, has_side_effects=True, vmem_limit_bytes=56 * 1024 * 1024
        ),
        name="relax_far_gram",
    )(
        field,
        block_inverse.reshape(PLANES, 9, NODES),
        face_weight.reshape(PLANES, 6, NODES),
        mixing.reshape(54),
        far_tiles.reshape(PLANES, 3, NODES, NODES),
        far_column.reshape(PLANES, 3),
        labels,
    )

    packed, inverse = pl.pallas_call(
        factor_kernel,
        out_shape=(
            jax.ShapeDtypeStruct((slots_total, K * K), jnp.float32),
            jax.ShapeDtypeStruct((TRI, 3 * WIDTH), bf16),
        ),
        in_specs=[whole, whole],
        out_specs=(whole, whole),
        scratch_shapes=[vmem((K * K, WIDTH)), vmem((TRI, WIDTH))],
        compiler_params=pltpu.CompilerParams(vmem_limit_bytes=32 * 1024 * 1024),
        name="factor",
    )(gram, table)

    received = lax.all_to_all(
        packed.reshape(n_wide * n_narrow, SLOT, K * K), ("wide", "narrow"), split_axis=0, concat_axis=0, tiled=True
    )

    projected = pl.pallas_call(
        project_kernel,
        grid=(PLANES,),
        out_shape=jax.ShapeDtypeStruct((PLANES, ROWS, NODES), jnp.float32),
        in_specs=[
            pl.BlockSpec((1, ROWS, NODES), lambda r: (r, 0, 0)),
            pl.BlockSpec((1, 1, NODES), lambda r: (r, 0, 0)),
            whole,
        ],
        out_specs=pl.BlockSpec((1, ROWS, NODES), lambda r: (r, 0, 0)),
        scratch_shapes=[vmem((TRI, NODES))],
        compiler_params=pltpu.CompilerParams(vmem_limit_bytes=32 * 1024 * 1024),
        cost_estimate=pl.CostEstimate(flops=8_000_000_000, bytes_accessed=4_000_000, transcendentals=0),
        name="project",
    )(combined, labels, inverse)
    prolong = projected.reshape(PLANES, 3, K, NODES).transpose(0, 2, 1, 3).reshape(tests.shape)
    return prolong, received.reshape(1, slots_total, K * K)


def solution(mesh):
    in_specs = (
        P("wide", None, None, "narrow", None),
        P("wide", None, None, "narrow", None),
        P("wide", None, "narrow", None),
        P(),
        P("wide", "narrow", None, None, None),
        P("wide", "narrow", None),
        P("wide", "narrow", None),
        P(("wide", "narrow")),
    )
    out_specs = (P("wide", None, None, "narrow", None), P(("wide", "narrow"), None, None))
    body = functools.partial(shards, mesh.shape["wide"], mesh.shape["narrow"])
    return jax.shard_map(body, mesh=mesh, in_specs=in_specs, out_specs=out_specs, check_vma=False)
```

time: 640 us -> 122 us (0.19); the launches traced: 629 us -> 122 us
  other arithmetic: 205 us -> 1.6 us
  waiting for transfers between devices: 131 us -> 5.87 us
  local copies, waits for them, and re-layouts: 113 us -> 27.3 us
  matrix products: 78 us -> 0 us
  Pallas kernels: 0 us -> 71.2 us
  starting transfers between devices: 72.7 us -> 15 us
  between operations: 18 us -> 0.73 us
  blocking collectives: 10.1 us -> 0 us
    add x51 -> x0, other arithmetic: 150 us -> none  [the longest x25 129 us: mix_components(): matrix[component, 0] * field_values[:, :, 0]]
    dot_general x40 -> x0, matrix products: 78 us -> none  [the longest x16 32.4 us: gram_step(): jnp.dot(outer_sum, onehot, precision=highest)]
    pallas_call x0 -> x3, Pallas kernels: none -> 71.2 us  [the longest x1 64 us: shards(): pl.pallas_call(functools.partial(relax_kernel, n_wide), out_shape=(jax.Sh...]
    ppermute x18 -> x0, waiting for transfers between devices: 58.9 us -> none  [the longest x6 27.9 us: with_halo(): before = lax.ppermute(last, axis, up)]
    ppermute x18 -> x0, starting transfers between devices: 50.9 us -> none  [the longest x6 30.5 us: with_halo(): before = lax.ppermute(last, axis, up)]
    reduce_sum x111 -> x0, other arithmetic: 37.1 us -> none  [the longest x16 15.3 us: gram_step(): jnp.sum(onehot, axis=0)]
    unnamed x4 -> x0, waiting for transfers between devices: 36.7 us -> none
    all_to_all x3 -> x1, waiting for transfers between devices: 35.7 us -> 5.87 us  [shards(): lax.all_to_all(packed.reshape(n_wide * n_narrow, SLOT, K * K), ('wide', '...]
  transfers between devices with their start and end apart: 23 -> 1, of which waited for: 11 -> 1; matrix products, arithmetic and copies ran while one was open for 43% -> 5% of each run, Pallas kernels for 0% -> 4%
where the time goes in v1:
time: 122 us
  Pallas kernels  71.2 us (58%)
  local copies, waits for them, and re-layouts  27.3 us (22%)
  starting transfers between devices  15 us (12%)
  waiting for transfers between devices  5.87 us (5%)
  other arithmetic  1.6 us (1%)
    pallas_call x1, Pallas kernels, shards(): pl.pallas_call(functools.partial(relax_kernel, n_wide), out_shape=(jax.Sh...  64 us
    all_to_all x1, starting transfers between devices, shards(): lax.all_to_all(packed.reshape(n_wide * n_narrow, SLOT, K * K), ('wide', '...  15 us
    unnamed x12, local copies, waits for them, and re-layouts  7.69 us
    all_to_all x1, waiting for transfers between devices, shards(): lax.all_to_all(packed.reshape(n_wide * n_narrow, SLOT, K * K), ('wide', '...  5.87 us
    reshape x2, local copies, waits for them, and re-layouts, shards(): tests.reshape(PLANES, K, 3, NODES).transpose(0, 2, 1, 3)  5.56 us
    pallas_call x1, Pallas kernels, shards(): pl.pallas_call(project_kernel, grid=(PLANES,), out_shape=jax.ShapeDtypeSt...  5.4 us
    reshape x1, local copies, waits for them, and re-layouts, shards(): return (prolong, received.reshape(1, slots_total, K * K))  2.91 us
    reshape x1, local copies, waits for them, and re-layouts, shards(): projected.reshape(PLANES, 3, K, NODES).transpose(0, 2, 1, 3)  2.51 us
  transfers between devices with their start and end apart: 1, of which 1 were waited for; matrix products, arithmetic and copies ran while one was open for 5% of the time, Pallas kernels for 4%

profile of v1, /device:TPU:1, one launch (start us, length us, event | category | flops | bytes accessed | tf_op | source)
XLA Modules:
  0.0 121.7 jit_solution(16420548116123568946)
XLA Ops:
  0.6 0.9 convert_reduce_fusion
  1.5 0.7 multiply_add_fusion
  2.2 0.1 tile.10
  2.3 1.3 %copy.33 = s32[16,1,3]{2,0,1:T(8,128)} copy(s32[16,1,3]{0,1,2:T(1,128)} %param.13) | data formatting | bytes 384 | tf_op jit(solution)/shard_map/reshape | solution.py:392
  3.6 0.8 copy.25
  4.4 0.6 reshape.66.mix_ref
  5.0 1.4 %reshape.69.label_ref = s32[16,1,256]{2,1,0:T(1,128)} reshape(s32[16,4,64]{2,1,0:T(4,128)} %param.14) | data formatting | bytes 32768 | tf_op jit(solution)/shard_map/reshape | solution.py:337
  6.5 1.7 %reshape.76.fw_ref = f32[16,6,256]{2,1,0:T(8,128)} reshape(f32[16,6,4,64]{3,2,1,0:T(4,128)} %param.10) | data formatting | bytes 196608 | tf_op jit(solution)/shard_map/reshape | solution.py:389
  8.2 1.9 %reshape.75.bi_ref = f32[16,9,256]{2,1,0:T(8,128)} reshape(f32[16,3,3,4,64]{4,3,2,1,0:T(4,128)} %param.9) | data formatting | bytes 294912 | tf_op jit(solution)/shard_map/reshape | solution.py:388
  10.1 4.1 %reshape.74 = f32[16,32,3,256]{3,2,1,0:T(4,128)S(1)} reshape(f32[16,32,3,4,64]{4,3,2,1,0:T(4,128)} %param.8) | data formatting | bytes 3145728 | tf_op jit(solution)/shard_map/reshape | solution.py:336
  14.3 1.4 %copy.30 = f32[16,32,3,256]{3,1,2,0:T(8,128)} copy(f32[16,32,3,256]{3,2,1,0:T(4,128)S(1)} %reshape.74) | data formatting | bytes 3145728 | tf_op jit(solution)/shard_map/reshape | solution.py:336
  15.7 64.0 %relax_far_gram.1 = (f32[16,96,256]{2,1,0:T(8,128)}, f32[656,128]{1,0:T(8,128)}) custom-call(f32[16,96,256]{2,1,0:T(8,128)} %bitcast.13, f32[16,9,256]{2,1,0:T(8,128)} %reshape.75.bi_ref, f32[16,6,256]{2,1,0:T(8,128)} %reshape.76.fw_ref, f32[54]{0:T(128)} %reshape.66.mix_ref, bf16[16,3,256,256]{3,2,1,0:T(8,128)(2,1)} %bitcast.14, s32[16,3]{1,0:T(8,128)} %bitcast.15, ...), custom_call_target="tpu_custom_call" | custom-call | tf_op jit(solution)/shard_map/relax_far_gram/pallas_call | solution.py:349
  79.7 1.0 copy-done
  80.7 1.8 %factor.1 = (f32[256,1024]{1,0:T(8,128)S(1)}, bf16[640,384]{1,0:T(8,128)(2,1)S(1)}) custom-call(f32[656,128]{1,0:T(8,128)S(1)} %copy-done, bf16[256,128]{1,0:T(8,128)(2,1)S(1)} %fusion.table_ref), custom_call_target="tpu_custom_call" | custom-call | tf_op jit(solution)/shard_map/factor/pallas_call | solution.py:396
  82.5 0.8 copy-done.3
  83.2 1.6 %reshape.72 = f32[128,2,1024]{2,1,0:T(2,128)} reshape(f32[256,1024]{1,0:T(8,128)S(1)} %get-tuple-element.9) | data formatting | bytes 2097152 | tf_op jit(solution)/shard_map/reshape | solution.py:410
  84.8 15.0 %all-to-all-start = ((f32[128,2,1024]{2,1,0:T(2,128)}), f32[128,2,1024]{2,1,0:T(2,128)}, u32[]{:S(2)}, u32[]{:S(2)}) async-start(f32[128,2,1024]{2,1,0:T(2,128)} %reshape.72), calls=%async_computation | async-start | bytes 2097152 | tf_op jit(solution)/shard_map/all_to_all | solution.py:409
  99.9 0.0 copy-start.4
  99.9 1.0 copy-done.4
  100.9 5.4 %project.1 = f32[16,96,256]{2,1,0:T(8,128)S(1)} custom-call(f32[16,96,256]{2,1,0:T(8,128)S(1)} %copy-done.2, s32[16,1,256]{2,1,0:T(1,128)S(1)} %copy-done.1, bf16[640,384]{1,0:T(8,128)(2,1)S(1)} %copy-done.4), custom_call_target="tpu_custom_call" | custom-call | flops 8000000000 | bytes 4000000 | tf_op jit(solution)/shard_map/project/pallas_call | solution.py:413
  106.3 2.5 %reshape.71 = f32[16,32,3,4,64]{4,3,1,2,0:T(4,128)} reshape(f32[16,32,3,256]{3,1,2,0:T(8,128)S(1)} %bitcast.12) | data formatting | bytes 3145728 | tf_op jit(solution)/shard_map/reshape | solution.py:428
  108.8 4.1 %copy.29 = f32[16,32,3,4,64]{4,3,2,1,0:T(4,128)} copy(f32[16,32,3,4,64]{4,3,1,2,0:T(4,128)} %reshape.71) | data formatting | bytes 3145728
  112.9 5.9 %all-to-all-done = f32[128,2,1024]{2,1,0:T(2,128)} async-done(((f32[128,2,1024]{2,1,0:T(2,128)}), f32[128,2,1024]{2,1,0:T(2,128)}, u32[]{:S(2)}, u32[]{:S(2)}) %all-to-all-start) | async-done | bytes 1048608 | tf_op jit(solution)/shard_map/all_to_all | solution.py:409
  118.8 2.9 %reshape.73 = f32[1,256,1024]{2,1,0:T(8,128)} reshape(f32[128,2,1024]{2,1,0:T(2,128)} %all-to-all-done) | data formatting | bytes 2097152 | tf_op jit(solution)/shard_map/reshape | solution.py:429
  (9 shorter events, 0.0 us)
Async XLA Ops:
  79.7 1.0 copy-start
  80.7 19.2 %copy-start.1 = (s32[16,1,256]{2,1,0:T(1,128)S(1)}, s32[16,1,256]{2,1,0:T(1,128)}, u32[]{:S(2)}) copy-start(s32[16,1,256]{2,1,0:T(1,128)} %reshape.69.label_ref) | copy-start | bytes 49156
  80.7 19.2 %copy-start.2 = (f32[16,96,256]{2,1,0:T(8,128)S(1)}, f32[16,96,256]{2,1,0:T(8,128)}, u32[]{:S(2)}) copy-start(f32[16,96,256]{2,1,0:T(8,128)} %get-tuple-element.6.comb_ref) | copy-start | bytes 4718596
  82.5 0.8 copy-start.3
  84.8 34.0 %all-to-all-start = ((f32[128,2,1024]{2,1,0:T(2,128)}), f32[128,2,1024]{2,1,0:T(2,128)}, u32[]{:S(2)}, u32[]{:S(2)}) async-start(f32[128,2,1024]{2,1,0:T(2,128)} %reshape.72), calls=%async_computation | async-start | bytes 2097152 | tf_op jit(solution)/shard_map/all_to_all | solution.py:409
  99.9 1.0 copy-start.4

commit v2 on v1

--- a/solution.py
+++ b/solution.py
@@ -23,6 +23,8 @@
 for place, (block_k, block_b) in enumerate(BLOCKS):
     STARTS.setdefault(block_k, 8 * place)
 GRAM_ROWS = TRI + 16
+CHUNKS = 4
+PART = PLANES // CHUNKS
 
 
 def split3(x):
@@ -33,12 +35,17 @@
     return hi, mid, low
 
 
+def join_rows(rows):
+    return jnp.concatenate(rows, axis=1)
+
+
 def relax_kernel(
     n_wide,
     tests_hbm, bi_ref, fw_ref, mix_ref, tiles_hbm, col_ref, label_ref,
     comb_ref, gram_ref,
-    x0, x1, x2, coef, ysend, yrecv, ydup, from_left, planes, from_right, tiles, outer, acc, gram_in,
-    local_sems, xsend_sems, xrecv_sems, ysend_sems, yrecv_sems, psend_sems, precv_sems, gsend_sem, grecv_sem,
+    raw, x0, x1, x2, coef, ysend, yrecv, ydup, from_left, planes, from_right, tiles, members, outer, acc, gram_in,
+    tests_sems, tiles_sem, xsend_sems, xrecv_sems, ysend_sems, yrecv_sems, psend_sems, precv_sems, gsend_sems,
+    grecv_sems,
 ):
     w = lax.axis_index("wide")
     n = lax.axis_index("narrow")
@@ -47,18 +54,27 @@
     other = 1 - n
     fields = [x0, x1, x2]
 
-    tests_copy = pltpu.make_async_copy(tests_hbm, x0.at[pl.ds(1, PLANES)], local_sems.at[0])
-    tests_copy.start()
-    tiles_copy = pltpu.make_async_copy(tiles_hbm, tiles, local_sems.at[1])
+    def plane_at(i):
+        half = i // 2
+        return jnp.where(lax.rem(i, 2) == 0, half, PLANES - 1 - half)
+
+    tests_copies = []
+    for q in range(CHUNKS):
+        for j, start in enumerate((2 * q, PLANES - 2 - 2 * q)):
+            span = pl.ds(start, 2)
+            copy = pltpu.make_async_copy(tests_hbm.at[span], raw.at[span], tests_sems.at[2 * q + j])
+            copy.start()
+            tests_copies.append(copy)
+    tiles_copy = pltpu.make_async_copy(tiles_hbm, tiles, tiles_sem.at[0])
     tiles_copy.start()
 
     barrier = pltpu.get_barrier_semaphore()
     for target in ((left, n), (right, n), (w, other)):
         pl.semaphore_signal(barrier, inc=1, device_id=target, device_id_type=MESH)
-    pl.semaphore_wait(barrier, 3)
 
     lane = lax.broadcasted_iota(jnp.int32, (K + 16, WIDTH), 1)
     low_half = lane < 64
+    low8 = low_half[0:8]
     is_low = n == 0
 
     def pack_row(first, second):
@@ -68,10 +84,11 @@
         b = jnp.where(is_low, chosen, turned)[48:96]
         return jnp.where(low_half, a, b).astype(jnp.bfloat16)
 
-    def y_copy(s):
+    def y_copy(s, q):
+        span = pl.ds(q * PART, PART)
         return pltpu.make_async_remote_copy(
-            src_ref=ysend.at[s], dst_ref=yrecv.at[s], send_sem=ysend_sems.at[s], recv_sem=yrecv_sems.at[s],
-            device_id=(w, other), device_id_type=MESH,
+            src_ref=ysend.at[s, span], dst_ref=yrecv.at[s, span], send_sem=ysend_sems.at[s * CHUNKS + q],
+            recv_sem=yrecv_sems.at[s * CHUNKS + q], device_id=(w, other), device_id_type=MESH,
         )
 
     def x_copies(s):
@@ -85,22 +102,37 @@
         )
         return up, down
 
-    tests_copy.wait()
-
-    def pack_tests(p, carry):
-        ysend[0, p] = pack_row(x0[p + 1, :, 0:128], x0[p + 1, :, 128:256])
+    def start_x(s):
+        for copy in x_copies(s):
+            copy.start()
+
+    def unpack_tests(i, carry):
+        p = plane_at(i)
+        for c in range(3):
+            for kb in range(K // 8):
+                pieces = [raw[p, pl.ds(96 * kb + 4 * c + y, 8, stride=12), :] for y in range(4)]
+                x0[p + 1, pl.ds(c * K + 8 * kb, 8), :] = join_rows(pieces)
+        ysend[0, i] = pack_row(x0[p + 1, :, 0:128], x0[p + 1, :, 128:256])
         return carry
 
-    for copy in x_copies(0):
-        copy.start()
-    lax.fori_loop(0, PLANES, pack_tests, 0)
-    y_copy(0).start()
+    for q in range(CHUNKS):
+        tests_copies[2 * q].wait()
+        tests_copies[2 * q + 1].wait()
+        lax.fori_loop(q * PART, (q + 1) * PART, unpack_tests, 0)
+        if q == 0:
+            pl.semaphore_wait(barrier, 3)
+            start_x(0)
+        y_copy(0, q).start()
 
     lane_wide = lax.broadcasted_iota(jnp.int32, (8, NODES), 1)
     z_place = lax.rem(lane_wide, 64)
 
     def make_coef(p, carry):
-        inv_rows = [jnp.broadcast_to(bi_ref[p, i : i + 1, :], (8, NODES)) for i in range(9)]
+        def wide_row(ref, first):
+            row = join_rows([ref[pl.ds(first + y, 1), :] for y in range(4)])
+            return jnp.broadcast_to(row, (8, NODES))
+
+        inv_rows = [wide_row(bi_ref, 36 * p + 4 * i) for i in range(9)]
         edges = [
             jnp.logical_and(p == PLANES - 1, w == n_wide - 1),
             jnp.logical_and(p == 0, w == 0),
@@ -110,23 +142,24 @@
             z_place == 0,
         ]
         for d in range(6):
-            weight = 0.5 * jnp.broadcast_to(fw_ref[p, d : d + 1, :], (8, NODES))
-            weight = jnp.where(edges[d], 0.0, weight)
+            weight = jnp.where(edges[d], 0.0, 0.5 * wide_row(fw_ref, 24 * p + 4 * d))
             for a in range(3):
                 for b in range(3):
                     total = inv_rows[3 * a] * mix_ref[9 * d + b]
                     total += inv_rows[3 * a + 1] * mix_ref[9 * d + 3 + b]
                     total += inv_rows[3 * a + 2] * mix_ref[9 * d + 6 + b]
                     coef[p, 9 * d + 3 * a + b] = total * weight
+        label = join_rows([label_ref[pl.ds(4 * p + y, 1), :] for y in range(4)])
+        groups = lax.broadcasted_iota(jnp.int32, (WIDTH, NODES), 0)
+        members[p] = jnp.where(groups == label, 1.0, 0.0).astype(jnp.bfloat16)
         return carry
 
     lax.fori_loop(0, PLANES, make_coef, 0)
 
-    low8 = low_half[0:8]
-
-    def sweep_plane(s, p):
+    def sweep_plane(s, i):
+        p = plane_at(i)
         src = fields[s]
-        packed = yrecv[s, p].astype(jnp.float32)
+        packed = yrecv[s, i].astype(jnp.float32)
         turned = pltpu.roll(packed, 64, 1)
         ydup[0:48] = jnp.where(low_half, packed, turned)
         ydup[48:96] = jnp.where(low_half, turned, packed)
@@ -156,60 +189,49 @@
                     fields[s + 1][p + 1, rows, :] = total
                 else:
                     comb_ref[p, rows, :] = total
-
-    def wait_sweep(s):
+        if s + 1 < SWEEPS:
+            ysend[s + 1, i] = pack_row(fields[s + 1][p + 1, :, 0:128], fields[s + 1][p + 1, :, 128:256])
+        else:
+            planes[p] = comb_ref[p].astype(jnp.bfloat16)
+
+    def plane_copies(q):
+        copies = []
+        for j, start in enumerate((2 * q, PLANES - 2 - 2 * q)):
+            span = pl.ds(start, 2)
+            for side, (target, landing) in enumerate(((right, from_left), (left, from_right))):
+                at = 4 * q + 2 * j + side
+                copies.append(
+                    pltpu.make_async_remote_copy(
+                        src_ref=planes.at[span], dst_ref=landing.at[span], send_sem=psend_sems.at[at],
+                        recv_sem=precv_sems.at[at], device_id=(target, n), device_id_type=MESH,
+                    )
+                )
+        return copies
+
+    for s in range(SWEEPS):
         for copy in x_copies(s):
             copy.wait()
-        y_copy(s).wait()
-
-    for s in range(SWEEPS - 1):
-        wait_sweep(s)
-
-        def one_plane(p, carry, s=s):
-            sweep_plane(s, p)
-            ysend[s + 1, p] = pack_row(fields[s + 1][p + 1, :, 0:128], fields[s + 1][p + 1, :, 128:256])
+
+        def one_chunk(q, carry, s=s):
+            y_copy(s, q).wait()
+
+            def one_plane(j, inner):
+                sweep_plane(s, q * PART + j)
+                if s + 1 < SWEEPS:
+                    pl.when(jnp.logical_and(q == 0, j == 1))(lambda: start_x(s + 1))
+                return inner
+
+            lax.fori_loop(0, PART, one_plane, 0)
+            if s + 1 < SWEEPS:
+                y_copy(s + 1, q).start()
+            else:
+                for copy in plane_copies(q):
+                    copy.start()
             return carry
 
-        lax.fori_loop(0, PLANES, one_plane, 0)
-        for copy in x_copies(s + 1):
-            copy.start()
-        y_copy(s + 1).start()
-
-    wait_sweep(SWEEPS - 1)
-    chunk_planes = 4
-    chunks = PLANES // chunk_planes
-
-    def plane_copies(q):
-        span = pl.ds(q * chunk_planes, chunk_planes)
-        up = pltpu.make_async_remote_copy(
-            src_ref=planes.at[span], dst_ref=from_left.at[span], send_sem=psend_sems.at[2 * q],
-            recv_sem=precv_sems.at[2 * q], device_id=(right, n), device_id_type=MESH,
-        )
-        down = pltpu.make_async_remote_copy(
-            src_ref=planes.at[span], dst_ref=from_right.at[span], send_sem=psend_sems.at[2 * q + 1],
-            recv_sem=precv_sems.at[2 * q + 1], device_id=(left, n), device_id_type=MESH,
-        )
-        return up, down
-
-    for q in range(chunks):
-
-        def last_plane(p, carry):
-            sweep_plane(SWEEPS - 1, p)
-            planes[p] = comb_ref[p].astype(jnp.bfloat16)
-            return carry
-
-        lax.fori_loop(q * chunk_planes, (q + 1) * chunk_planes, last_plane, 0)
-        for copy in plane_copies(q):
-            copy.start()
+        lax.fori_loop(0, CHUNKS, one_chunk, 0)
 
     tiles_copy.wait()
-
-    acc[...] = jnp.zeros_like(acc)
-    ones = jnp.ones((16, NODES), jnp.bfloat16)
-    outer[0, TRI:GRAM_ROWS] = ones
-    outer[1, TRI:GRAM_ROWS] = jnp.zeros_like(ones)
-    outer[2, TRI:GRAM_ROWS] = jnp.zeros_like(ones)
-
     sources = [from_left, planes, from_right]
 
     def far_product(r, slot):
@@ -223,43 +245,65 @@
 
     lax.fori_loop(0, PLANES, near_far, 0)
 
-    for q in range(chunks):
+    acc[...] = jnp.zeros_like(acc)
+    for q in range(CHUNKS):
         for copy in plane_copies(q):
             copy.wait()
 
-    groups = lax.broadcasted_iota(jnp.int32, (WIDTH, NODES), 0)
-
-    def gram_plane(r, carry):
+    def side_far(r, carry):
         comb_ref[r] = comb_ref[r] + (far_product(r, 0) + far_product(r, 2))
-        member = jnp.where(groups == label_ref[r], 1.0, 0.0).astype(jnp.bfloat16)
-        for pair in range(len(BLOCKS) // 2):
-            parts = []
-            for k, b in BLOCKS[2 * pair : 2 * pair + 2]:
-                value = None
-                for c in range(3):
-                    term = comb_ref[r, c * K + k : c * K + k + 1, :] * comb_ref[r, pl.ds(c * K + 8 * b, 8), :]
-                    value = term if value is None else value + term
-                parts.append(value)
-            pieces = split3(jnp.concatenate(parts, axis=0))
-            for i in range(3):
-                outer[i, pl.ds(16 * pair, 16), :] = pieces[i]
-        total = None
-        for i in range(3):
-            term = lax.dot_general(
-                outer[i], member, (((1,), (1,)), ((), ())), preferred_element_type=jnp.float32
-            )
-            total = term if total is None else total + term
-        acc[...] += total
         return carry
 
-    lax.fori_loop(0, PLANES, gram_plane, 0)
-
-    gram_copy = pltpu.make_async_remote_copy(
-        src_ref=acc, dst_ref=gram_in, send_sem=gsend_sem.at[0], recv_sem=grecv_sem.at[0],
-        device_id=(w, other), device_id_type=MESH,
-    )
-    gram_copy.start()
-    gram_copy.wait()
+    lax.fori_loop(0, PLANES, side_far, 0)
+
+    pairs = len(BLOCKS) // 2 // CHUNKS
+    rows_part = 16 * pairs
+
+    def gram_copy(t):
+        height = rows_part if t + 1 < CHUNKS else GRAM_ROWS - rows_part * t
+        span = pl.ds(rows_part * t, height)
+        return pltpu.make_async_remote_copy(
+            src_ref=acc.at[span], dst_ref=gram_in.at[span], send_sem=gsend_sems.at[t], recv_sem=grecv_sems.at[t],
+            device_id=(w, other), device_id_type=MESH,
+        )
+
+    def contract(values, member):
+        return lax.dot_general(values, member, (((1,), (1,)), ((), ())), preferred_element_type=jnp.float32)
+
+    for t in range(CHUNKS):
+
+        def gram_planes(h, carry, t=t):
+            for side in range(2):
+                r = 2 * h + side
+                lanes = pl.ds(side * NODES, NODES)
+                for pair in range(pairs):
+                    parts = []
+                    for k, b in BLOCKS[2 * (pairs * t + pair) : 2 * (pairs * t + pair) + 2]:
+                        value = None
+                        for c in range(3):
+                            term = comb_ref[r, c * K + k : c * K + k + 1, :] * comb_ref[r, pl.ds(c * K + 8 * b, 8), :]
+                            value = term if value is None else value + term
+                        parts.append(value)
+                    for piece, values in enumerate(split3(jnp.concatenate(parts, axis=0))):
+                        outer[piece, pl.ds(16 * pair, 16), lanes] = values
+            total = None
+            for side in range(2):
+                member = members[2 * h + side]
+                lanes = pl.ds(side * NODES, NODES)
+                for piece in range(3):
+                    term = contract(outer[piece, :, lanes], member)
+                    total = term if total is None else total + term
+            acc[pl.ds(rows_part * t, rows_part), :] += total
+            if t + 1 == CHUNKS:
+                ones = jnp.ones((16, NODES), jnp.bfloat16)
+                acc[TRI:GRAM_ROWS] += contract(ones, members[2 * h]) + contract(ones, members[2 * h + 1])
+            return carry
+
+        lax.fori_loop(0, PLANES // 2, gram_planes, 0)
+        gram_copy(t).start()
+
+    for t in range(CHUNKS):
+        gram_copy(t).wait()
     gram_ref[...] = acc[...] + gram_in[...]
 
 
@@ -309,7 +353,9 @@
 
 def project_kernel(comb_ref, label_ref, inverse_ref, out_ref, look):
     groups = lax.broadcasted_iota(jnp.int32, (WIDTH, NODES), 0)
-    member = jnp.where(groups == label_ref[0], 1.0, 0.0).astype(jnp.bfloat16)
+    r = pl.program_id(0)
+    label = join_rows([label_ref[pl.ds(4 * r + y, 1), :] for y in range(4)])
+    member = jnp.where(groups == label, 1.0, 0.0).astype(jnp.bfloat16)
     look[...] = jnp.dot(
         inverse_ref[...], jnp.concatenate([member, member, member], axis=0), preferred_element_type=jnp.float32
     )
@@ -321,7 +367,8 @@
                 term = weight * comb_ref[0, c * K + l : c * K + l + 1, :]
                 totals[c] = term if totals[c] is None else totals[c] + term
         for c in range(3):
-            out_ref[0, pl.ds(c * K + 8 * b, 8), :] = totals[c]
+            for y in range(4):
+                out_ref[0, pl.ds(96 * b + 4 * c + y, 8, stride=12), :] = totals[c][:, 64 * y : 64 * (y + 1)]
 
 
 def vmem(shape, dtype=jnp.float32):
@@ -333,8 +380,7 @@
     whole = pl.BlockSpec(memory_space=pltpu.VMEM)
     any_spec = pl.BlockSpec(memory_space=pl.ANY)
     smem = pl.BlockSpec(memory_space=pltpu.SMEM)
-    field = tests.reshape(PLANES, K, 3, NODES).transpose(0, 2, 1, 3).reshape(PLANES, ROWS, NODES)
-    labels = aggregate.reshape(PLANES, 1, NODES)
+    labels = aggregate.reshape(PLANES * 4, 64)
 
     agg_dev = owner_map.shape[0]
     slot_order = jnp.arange(agg_dev, dtype=jnp.int32)
@@ -355,6 +401,7 @@
         in_specs=[any_spec, whole, whole, smem, any_spec, smem, whole],
         out_specs=(whole, whole),
         scratch_shapes=[
+            vmem((PLANES, 4 * ROWS, 64)),
             vmem((PLANES + 2, ROWS, NODES)),
             vmem((PLANES + 2, ROWS, NODES)),
             vmem((PLANES + 2, ROWS, NODES)),
@@ -366,27 +413,29 @@
             vmem((PLANES, ROWS, NODES), bf16),
             vmem((PLANES, ROWS, NODES), bf16),
             vmem((PLANES, 3, NODES, NODES), bf16),
-            vmem((3, GRAM_ROWS, NODES), bf16),
+            vmem((PLANES, WIDTH, NODES), bf16),
+            vmem((3, TRI // CHUNKS, 2 * NODES), bf16),
             vmem((GRAM_ROWS, WIDTH)),
             vmem((GRAM_ROWS, WIDTH)),
-            pltpu.SemaphoreType.DMA((2,)),
+            pltpu.SemaphoreType.DMA((2 * CHUNKS,)),
+            pltpu.SemaphoreType.DMA((1,)),
             pltpu.SemaphoreType.DMA((2 * SWEEPS,)),
             pltpu.SemaphoreType.DMA((2 * SWEEPS,)),
-            pltpu.SemaphoreType.DMA((SWEEPS,)),
-            pltpu.SemaphoreType.DMA((SWEEPS,)),
-            pltpu.SemaphoreType.DMA((8,)),
-            pltpu.SemaphoreType.DMA((8,)),
-            pltpu.SemaphoreType.DMA((1,)),
-            pltpu.SemaphoreType.DMA((1,)),
+            pltpu.SemaphoreType.DMA((SWEEPS * CHUNKS,)),
+            pltpu.SemaphoreType.DMA((SWEEPS * CHUNKS,)),
+            pltpu.SemaphoreType.DMA((4 * CHUNKS,)),
+            pltpu.SemaphoreType.DMA((4 * CHUNKS,)),
+            pltpu.SemaphoreType.DMA((CHUNKS,)),
+            pltpu.SemaphoreType.DMA((CHUNKS,)),
         ],
         compiler_params=pltpu.CompilerParams(
             collective_id=0, has_side_effects=True, vmem_limit_bytes=56 * 1024 * 1024
         ),
         name="relax_far_gram",
     )(
-        field,
-        block_inverse.reshape(PLANES, 9, NODES),
-        face_weight.reshape(PLANES, 6, NODES),
+        tests.reshape(PLANES, 4 * ROWS, 64),
+        block_inverse.reshape(PLANES * 36, 64),
+        face_weight.reshape(PLANES * 24, 64),
         mixing.reshape(54),
         far_tiles.reshape(PLANES, 3, NODES, NODES),
         far_column.reshape(PLANES, 3),
@@ -413,19 +462,15 @@
     projected = pl.pallas_call(
         project_kernel,
         grid=(PLANES,),
-        out_shape=jax.ShapeDtypeStruct((PLANES, ROWS, NODES), jnp.float32),
-        in_specs=[
-            pl.BlockSpec((1, ROWS, NODES), lambda r: (r, 0, 0)),
-            pl.BlockSpec((1, 1, NODES), lambda r: (r, 0, 0)),
-            whole,
-        ],
-        out_specs=pl.BlockSpec((1, ROWS, NODES), lambda r: (r, 0, 0)),
+        out_shape=jax.ShapeDtypeStruct((PLANES, 4 * ROWS, 64), jnp.float32),
+        in_specs=[pl.BlockSpec((1, ROWS, NODES), lambda r: (r, 0, 0)), whole, whole],
+        out_specs=pl.BlockSpec((1, 4 * ROWS, 64), lambda r: (r, 0, 0)),
         scratch_shapes=[vmem((TRI, NODES))],
         compiler_params=pltpu.CompilerParams(vmem_limit_bytes=32 * 1024 * 1024),
         cost_estimate=pl.CostEstimate(flops=8_000_000_000, bytes_accessed=4_000_000, transcendentals=0),
         name="project",
     )(combined, labels, inverse)
-    prolong = projected.reshape(PLANES, 3, K, NODES).transpose(0, 2, 1, 3).reshape(tests.shape)
+    prolong = projected.reshape(tests.shape)
     return prolong, received.reshape(1, slots_total, K * K)
 
 

time: 122 us -> 101 us (0.83)
  local copies, waits for them, and re-layouts: 27.3 us -> 7.1 us
  waiting for transfers between devices: 5.87 us -> 9.63 us
  Pallas kernels: 71.2 us -> 68.1 us
  starting transfers between devices: 15 us -> 13.5 us
    reshape x6 -> x0, local copies, waits for them, and re-layouts: 13.1 us -> none  [the longest x2 5.56 us: shards(): tests.reshape(PLANES, K, 3, NODES).transpose(0, 2, 1, 3)]
    pallas_call x1, Pallas kernels: 64 us -> 56.6 us  [shards(): pl.pallas_call(functools.partial(relax_kernel, n_wide), out_shape=(jax.Sh...]
    unnamed x12 -> x7, local copies, waits for them, and re-layouts: 7.69 us -> 1.77 us
    pallas_call x1, Pallas kernels: 5.4 us -> 9.66 us  [shards(): pl.pallas_call(project_kernel, grid=(PLANES,), out_shape=jax.ShapeDtypeSt...]
    all_to_all x1, waiting for transfers between devices: 5.87 us -> 9.63 us  [shards(): lax.all_to_all(packed.reshape(n_wide * n_narrow, SLOT, K * K), ('wide', '...]
    all_to_all x1, starting transfers between devices: 15 us -> 13.5 us  [shards(): lax.all_to_all(packed.reshape(n_wide * n_narrow, SLOT, K * K), ('wide', '...]
    reshape x1, local copies, waits for them, and re-layouts: 2.91 us -> 1.69 us  [shards(): return (prolong, received.reshape(1, slots_total, K * K))]
  transfers between devices with their start and end apart: 1 -> 1, of which waited for: 1 -> 1; matrix products, arithmetic and copies ran while one was open for 5% -> 0% of each run, Pallas kernels for 4% -> 10%
where the time goes in v2:
time: 101 us
  Pallas kernels  68.1 us (67%)
  starting transfers between devices  13.5 us (13%)
  waiting for transfers between devices  9.63 us (10%)
  local copies, waits for them, and re-layouts  7.1 us (7%)
  other arithmetic  1.6 us (2%)
    pallas_call x1, Pallas kernels, shards(): pl.pallas_call(functools.partial(relax_kernel, n_wide), out_shape=(jax.Sh...  56.6 us
    all_to_all x1, starting transfers between devices, shards(): lax.all_to_all(packed.reshape(n_wide * n_narrow, SLOT, K * K), ('wide', '...  13.5 us
    pallas_call x1, Pallas kernels, shards(): pl.pallas_call(project_kernel, grid=(PLANES,), out_shape=jax.ShapeDtypeSt...  9.66 us
    all_to_all x1, waiting for transfers between devices, shards(): lax.all_to_all(packed.reshape(n_wide * n_narrow, SLOT, K * K), ('wide', '...  9.63 us
  transfers between devices with their start and end apart: 1, of which 1 were waited for; matrix products, arithmetic and copies ran while one was open for 0% of the time, Pallas kernels for 10%

profile of v2, /device:TPU:1, one launch (start us, length us, event | category | flops | bytes accessed | tf_op | source)
XLA Modules:
  0.0 100.6 jit_solution(7253743479026165249)
XLA Ops:
  0.6 0.9 convert_reduce_fusion
  1.5 0.7 multiply_add_fusion
  2.2 0.1 tile.10
  2.3 1.4 %copy.16 = s32[16,1,3]{2,0,1:T(8,128)} copy(s32[16,1,3]{0,1,2:T(1,128)} %param.13) | data formatting | bytes 384 | tf_op jit(solution)/shard_map/reshape | solution.py:441
  3.7 0.8 copy.14
  4.5 0.6 reshape.59.mix_ref
  5.1 56.6 %relax_far_gram.1 = (f32[16,96,256]{2,1,0:T(8,128)}, f32[656,128]{1,0:T(8,128)}) custom-call(f32[16,384,64]{2,1,0:T(8,128)} %bitcast.10, f32[576,64]{1,0:T(8,128)} %bitcast.11, f32[384,64]{1,0:T(8,128)} %bitcast.12, f32[54]{0:T(128)} %reshape.59.mix_ref, bf16[16,3,256,256]{3,2,1,0:T(8,128)(2,1)} %bitcast.9, s32[16,3]{1,0:T(8,128)} %bitcast.13, s32[64,64]{1,0:T(8,128)} %bitcast.7), custom_call_target="tpu_custom_call" | custom-call | tf_op jit(solution)/shard_map/relax_far_gram/pallas_call | solution.py:395
  61.7 0.0 copy-start
  61.7 1.0 copy-done
  62.7 0.0 copy-start.1
  62.7 0.0 copy-start.2
  62.7 1.8 %factor.1 = (f32[256,1024]{1,0:T(8,128)S(1)}, bf16[640,384]{1,0:T(8,128)(2,1)S(1)}) custom-call(f32[656,128]{1,0:T(8,128)S(1)} %copy-done, bf16[256,128]{1,0:T(8,128)(2,1)S(1)} %fusion.table_ref), custom_call_target="tpu_custom_call" | custom-call | tf_op jit(solution)/shard_map/factor/pallas_call | solution.py:445
  64.5 1.6 %reshape.64 = f32[128,2,1024]{2,1,0:T(2,128)} reshape(f32[256,1024]{1,0:T(8,128)S(1)} %get-tuple-element.9) | data formatting | bytes 2097152 | tf_op jit(solution)/shard_map/reshape | solution.py:459
  66.1 13.5 %all-to-all-start = ((f32[128,2,1024]{2,1,0:T(2,128)}), f32[128,2,1024]{2,1,0:T(2,128)S(1)}, u32[]{:S(2)}, u32[]{:S(2)}) async-start(f32[128,2,1024]{2,1,0:T(2,128)} %reshape.64), calls=%async_computation | async-start | bytes 2097152 | tf_op jit(solution)/shard_map/all_to_all | solution.py:458
  79.6 0.0 copy-done.1
  79.6 0.0 copy-done.2
  79.6 9.7 %project.1 = f32[16,384,64]{2,1,0:T(8,128)} custom-call(f32[16,96,256]{2,1,0:T(8,128)S(1)} %copy-done.2, s32[64,64]{1,0:T(8,128)S(1)} %bitcast.8, bf16[640,384]{1,0:T(8,128)(2,1)S(1)} %get-tuple-element.8.inverse_ref), custom_call_target="tpu_custom_call" | custom-call | flops 8000000000 | bytes 4000000 | tf_op jit(solution)/shard_map/project/pallas_call | solution.py:462
  89.3 9.6 %all-to-all-done = f32[128,2,1024]{2,1,0:T(2,128)S(1)} async-done(((f32[128,2,1024]{2,1,0:T(2,128)}), f32[128,2,1024]{2,1,0:T(2,128)S(1)}, u32[]{:S(2)}, u32[]{:S(2)}) %all-to-all-start) | async-done | bytes 1048608 | tf_op jit(solution)/shard_map/all_to_all | solution.py:458
  98.9 1.7 %reshape.65 = f32[1,256,1024]{2,1,0:T(8,128)} reshape(f32[128,2,1024]{2,1,0:T(2,128)S(1)} %all-to-all-done) | data formatting | bytes 2097152 | tf_op jit(solution)/shard_map/reshape | solution.py:474
  (3 shorter events, 0.0 us)
Async XLA Ops:
  61.7 1.0 copy-start
  62.7 16.9 %copy-start.1 = (s32[16,4,64]{2,1,0:T(4,128)S(1)}, s32[16,4,64]{2,1,0:T(4,128)}, u32[]{:S(2)}) copy-start(s32[16,4,64]{2,1,0:T(4,128)} %param.14) | copy-start | bytes 49156
  62.7 16.9 %copy-start.2 = (f32[16,96,256]{2,1,0:T(8,128)S(1)}, f32[16,96,256]{2,1,0:T(8,128)}, u32[]{:S(2)}) copy-start(f32[16,96,256]{2,1,0:T(8,128)} %get-tuple-element.6.comb_ref) | copy-start | bytes 4718596
  66.1 32.9 %all-to-all-start = ((f32[128,2,1024]{2,1,0:T(2,128)}), f32[128,2,1024]{2,1,0:T(2,128)S(1)}, u32[]{:S(2)}, u32[]{:S(2)}) async-start(f32[128,2,1024]{2,1,0:T(2,128)} %reshape.64), calls=%async_computation | async-start | bytes 2097152 | tf_op jit(solution)/shard_map/all_to_all | solution.py:458

commit v3 on v2

--- a/solution.py
+++ b/solution.py
@@ -145,9 +145,9 @@
             weight = jnp.where(edges[d], 0.0, 0.5 * wide_row(fw_ref, 24 * p + 4 * d))
             for a in range(3):
                 for b in range(3):
-                    total = inv_rows[3 * a] * mix_ref[9 * d + b]
-                    total += inv_rows[3 * a + 1] * mix_ref[9 * d + 3 + b]
-                    total += inv_rows[3 * a + 2] * mix_ref[9 * d + 6 + b]
+                    total = inv_rows[3 * a] * mix_ref[0, b, d]
+                    total += inv_rows[3 * a + 1] * mix_ref[1, b, d]
+                    total += inv_rows[3 * a + 2] * mix_ref[2, b, d]
                     coef[p, 9 * d + 3 * a + b] = total * weight
         label = join_rows([label_ref[pl.ds(4 * p + y, 1), :] for y in range(4)])
         groups = lax.broadcasted_iota(jnp.int32, (WIDTH, NODES), 0)
@@ -236,7 +236,7 @@
 
     def far_product(r, slot):
         return jnp.dot(
-            sources[slot][col_ref[r, slot]], tiles[r, slot], preferred_element_type=jnp.float32
+            sources[slot][col_ref[slot, 0, r]], tiles[r, slot], preferred_element_type=jnp.float32
         )
 
     def near_far(r, carry):
@@ -307,7 +307,23 @@
     gram_ref[...] = acc[...] + gram_in[...]
 
 
-def factor_kernel(gram_ref, table_ref, packed_ref, inverse_ref, lower, inv):
+def slot_table(owner_ref, slots_total):
+    count = owner_ref.shape[1]
+    owners = owner_ref[...].astype(jnp.float32)
+    across = jnp.broadcast_to(owners, (count, count))
+    row = lax.broadcasted_iota(jnp.int32, (count, count), 0)
+    column = lax.broadcasted_iota(jnp.int32, (count, count), 1)
+    down = jnp.sum(jnp.where(row == column, across, 0.0), axis=1, keepdims=True)
+    earlier = jnp.where(jnp.logical_and(down == across, row < column), 1.0, 0.0)
+    target = owners * SLOT + jnp.sum(earlier, axis=0, keepdims=True)
+    none = jnp.full_like(target, -1.0)
+    is_low = lax.axis_index("narrow") == 0
+    lanes = join_rows([jnp.where(is_low, target, none), jnp.where(is_low, none, target)])
+    slots = lax.broadcasted_iota(jnp.int32, (slots_total, WIDTH), 0).astype(jnp.float32)
+    return jnp.where(slots == lanes, 1.0, 0.0).astype(jnp.bfloat16)
+
+
+def factor_kernel(gram_ref, owner_ref, packed_ref, inverse_ref, lower, inv):
     scale = 1.0 / (3.0 * gram_ref[TRI : TRI + 1, :])
     row = lax.broadcasted_iota(jnp.int32, (K, WIDTH), 0)
     columns = []
@@ -328,9 +344,7 @@
         for m in range(k + 1, K):
             begin = 8 * (m // 8)
             columns[m] = columns[m] - column[m - first : m - first + 1] * column[begin - first :]
-        lower[pl.ds(K * k, K), :] = (
-            column if first == 0 else jnp.concatenate([jnp.zeros((first, WIDTH), jnp.float32), column], axis=0)
-        )
+        lower[pl.ds(STARTS[k], K - first), :] = column
     for l in range(K):
         first = 8 * (l // 8)
         solved = jnp.where(row[first:] == l, 1.0, 0.0)
@@ -343,7 +357,7 @@
         inv[pl.ds(STARTS[l], K - first), :] = solved
     for i, piece in enumerate(split3(inv[...])):
         inverse_ref[:, i * WIDTH : (i + 1) * WIDTH] = piece
-    table = table_ref[...]
+    table = slot_table(owner_ref, packed_ref.shape[0])
     total = None
     for piece in split3(lower[...]):
         term = lax.dot_general(table, piece, (((1,), (1,)), ((), ())), preferred_element_type=jnp.float32)
@@ -351,24 +365,95 @@
     packed_ref[...] = total
 
 
-def project_kernel(comb_ref, label_ref, inverse_ref, out_ref, look):
+def project_kernel(
+    n_wide, n_narrow, packed_ref, comb_ref, label_ref, inverse_ref, out_ref, received_ref, landing, look, spare,
+    send_sem, recv_sem,
+):
+    count = n_wide * n_narrow
+    w = lax.axis_index("wide")
+    n = lax.axis_index("narrow")
+    me = w * n_narrow + n
+    barrier = pltpu.get_barrier_semaphore()
+
+    def peer(i):
+        index = lax.rem(me + i, count)
+        return index, (index // n_narrow, lax.rem(index, n_narrow))
+
+    def greet(i, carry):
+        pl.semaphore_signal(barrier, inc=1, device_id=peer(i)[1], device_id_type=MESH)
+        return carry
+
+    lax.fori_loop(1, count, greet, 0)
+    own_span = pl.ds(SLOT * me, SLOT)
+    pltpu.make_async_copy(packed_ref.at[own_span], landing.at[own_span], recv_sem).start()
+    pltpu.make_async_copy(packed_ref.at[own_span], spare, send_sem).start()
+
     groups = lax.broadcasted_iota(jnp.int32, (WIDTH, NODES), 0)
-    r = pl.program_id(0)
-    label = join_rows([label_ref[pl.ds(4 * r + y, 1), :] for y in range(4)])
-    member = jnp.where(groups == label, 1.0, 0.0).astype(jnp.bfloat16)
-    look[...] = jnp.dot(
-        inverse_ref[...], jnp.concatenate([member, member, member], axis=0), preferred_element_type=jnp.float32
+
+    def project_plane(r, carry):
+        label = join_rows([label_ref[pl.ds(4 * r + y, 1), :] for y in range(4)])
+        member = jnp.where(groups == label, 1.0, 0.0).astype(jnp.bfloat16)
+        look[...] = jnp.dot(
+            inverse_ref[...], jnp.concatenate([member, member, member], axis=0), preferred_element_type=jnp.float32
+        )
+        for b in range(K // 8):
+            totals = [None] * 3
+            for l in range(8 * (b + 1)):
+                weight = look[pl.ds(STARTS[l] + 8 * (b - l // 8), 8), :]
+                for c in range(3):
+                    term = weight * comb_ref[r, c * K + l : c * K + l + 1, :]
+                    totals[c] = term if totals[c] is None else totals[c] + term
+            for c in range(3):
+                for y in range(4):
+                    out_ref[r, pl.ds(96 * b + 4 * c + y, 8, stride=12), :] = totals[c][:, 64 * y : 64 * (y + 1)]
+        return carry
+
+    lax.fori_loop(0, PART, project_plane, 0)
+    pl.semaphore_wait(barrier, count - 1)
+
+    def send(i, carry):
+        index, device = peer(i)
+        pltpu.make_async_remote_copy(
+            src_ref=packed_ref.at[pl.ds(SLOT * index, SLOT)], dst_ref=landing.at[own_span], send_sem=send_sem,
+            recv_sem=recv_sem, device_id=device, device_id_type=MESH,
+        ).start()
+        return carry
+
+    lax.fori_loop(1, count, send, 0)
+    lax.fori_loop(PART, PLANES, project_plane, 0)
+    everything = pltpu.make_async_remote_copy(
+        src_ref=packed_ref, dst_ref=landing, send_sem=send_sem, recv_sem=recv_sem, device_id=peer(1)[1],
+        device_id_type=MESH,
     )
-    for b in range(K // 8):
-        totals = [None] * 3
-        for l in range(8 * (b + 1)):
-            weight = look[pl.ds(STARTS[l] + 8 * (b - l // 8), 8), :]
-            for c in range(3):
-                term = weight * comb_ref[0, c * K + l : c * K + l + 1, :]
-                totals[c] = term if totals[c] is None else totals[c] + term
-        for c in range(3):
-            for y in range(4):
-                out_ref[0, pl.ds(96 * b + 4 * c + y, 8, stride=12), :] = totals[c][:, 64 * y : 64 * (y + 1)]
+    everything.wait_send()
+    everything.wait_recv()
+    received_ref[...] = landing[...]
+
+
+def widen_kernel(received_ref, prolong_in, basis_ref, prolong_out, sem):
+    copy = pltpu.make_async_copy(prolong_in, prolong_out, sem)
+    copy.start()
+    pieces = split3(received_ref[...])
+    for m in range(K * K // WIDTH):
+        group = m // 2
+        width = K - 8 * group
+        start = STARTS[8 * group]
+        first = STARTS[4 * m] // WIDTH * WIDTH
+        last = -(-(STARTS[4 * m] + 4 * width) // WIDTH) * WIDTH
+        if group == 0:
+            basis_ref[0, :, WIDTH * m : WIDTH * (m + 1)] = received_ref[:, first:last]
+            continue
+        source = lax.broadcasted_iota(jnp.int32, (last - first, WIDTH), 0) + first
+        column = lax.broadcasted_iota(jnp.int32, (last - first, WIDTH), 1) + WIDTH * m
+        k, l = column // K, lax.rem(column, K)
+        wanted = start + (k - 8 * group) * width + l - 8 * group
+        place = jnp.where(jnp.logical_and(source == wanted, l >= 8 * group), 1.0, 0.0).astype(jnp.bfloat16)
+        total = None
+        for piece in pieces:
+            term = jnp.dot(piece[:, first:last], place, preferred_element_type=jnp.float32)
+            total = term if total is None else total + term
+        basis_ref[0, :, WIDTH * m : WIDTH * (m + 1)] = total
+    copy.wait()
 
 
 def vmem(shape, dtype=jnp.float32):
@@ -382,16 +467,7 @@
     smem = pl.BlockSpec(memory_space=pltpu.SMEM)
     labels = aggregate.reshape(PLANES * 4, 64)
 
-    agg_dev = owner_map.shape[0]
-    slot_order = jnp.arange(agg_dev, dtype=jnp.int32)
-    same_owner = (owner_map[:, None] == owner_map[None, :]) & (slot_order[None, :] < slot_order[:, None])
-    within = jnp.sum(same_owner.astype(jnp.int32), axis=1)
-    target = owner_map * SLOT + within
     slots_total = n_wide * n_narrow * SLOT
-    own_lane = jnp.arange(WIDTH, dtype=jnp.int32) // agg_dev == lax.axis_index("narrow")
-    target_lane = jnp.where(own_lane, jnp.tile(target, n_narrow), -1)
-    table = (jnp.arange(slots_total, dtype=jnp.int32)[:, None] == target_lane[None, :]).astype(bf16)
-
     combined, gram = pl.pallas_call(
         functools.partial(relax_kernel, n_wide),
         out_shape=(
@@ -436,42 +512,59 @@
         tests.reshape(PLANES, 4 * ROWS, 64),
         block_inverse.reshape(PLANES * 36, 64),
         face_weight.reshape(PLANES * 24, 64),
-        mixing.reshape(54),
+        mixing.transpose(1, 2, 0),
         far_tiles.reshape(PLANES, 3, NODES, NODES),
-        far_column.reshape(PLANES, 3),
+        far_column.transpose(2, 1, 0),
         labels,
     )
 
     packed, inverse = pl.pallas_call(
         factor_kernel,
         out_shape=(
-            jax.ShapeDtypeStruct((slots_total, K * K), jnp.float32),
+            jax.ShapeDtypeStruct((slots_total, TRI), jnp.float32),
             jax.ShapeDtypeStruct((TRI, 3 * WIDTH), bf16),
         ),
         in_specs=[whole, whole],
         out_specs=(whole, whole),
-        scratch_shapes=[vmem((K * K, WIDTH)), vmem((TRI, WIDTH))],
+        scratch_shapes=[vmem((TRI, WIDTH)), vmem((TRI, WIDTH))],
         compiler_params=pltpu.CompilerParams(vmem_limit_bytes=32 * 1024 * 1024),
         name="factor",
-    )(gram, table)
-
-    received = lax.all_to_all(
-        packed.reshape(n_wide * n_narrow, SLOT, K * K), ("wide", "narrow"), split_axis=0, concat_axis=0, tiled=True
-    )
-
-    projected = pl.pallas_call(
-        project_kernel,
-        grid=(PLANES,),
-        out_shape=jax.ShapeDtypeStruct((PLANES, 4 * ROWS, 64), jnp.float32),
-        in_specs=[pl.BlockSpec((1, ROWS, NODES), lambda r: (r, 0, 0)), whole, whole],
-        out_specs=pl.BlockSpec((1, 4 * ROWS, 64), lambda r: (r, 0, 0)),
-        scratch_shapes=[vmem((TRI, NODES))],
+    )(gram, owner_map.reshape(1, owner_map.shape[0]))
+
+    projected, received = pl.pallas_call(
+        functools.partial(project_kernel, n_wide, n_narrow),
+        out_shape=(
+            jax.ShapeDtypeStruct((PLANES, 4 * ROWS, 64), jnp.float32),
+            jax.ShapeDtypeStruct((slots_total, TRI), jnp.float32),
+        ),
+        in_specs=[whole, whole, whole, whole],
+        out_specs=(whole, whole),
+        scratch_shapes=[
+            vmem((slots_total, TRI)),
+            vmem((TRI, NODES)),
+            vmem((SLOT, TRI)),
+            pltpu.SemaphoreType.DMA,
+            pltpu.SemaphoreType.DMA,
+        ],
+        compiler_params=pltpu.CompilerParams(
+            collective_id=1, has_side_effects=True, vmem_limit_bytes=40 * 1024 * 1024
+        ),
+        name="project",
+    )(packed, combined, labels, inverse)
+
+    basis, prolong = pl.pallas_call(
+        widen_kernel,
+        out_shape=(
+            jax.ShapeDtypeStruct((1, slots_total, K * K), jnp.float32),
+            jax.ShapeDtypeStruct((PLANES, 4 * ROWS, 64), jnp.float32),
+        ),
+        in_specs=[whole, any_spec],
+        out_specs=(whole, any_spec),
+        scratch_shapes=[pltpu.SemaphoreType.DMA],
         compiler_params=pltpu.CompilerParams(vmem_limit_bytes=32 * 1024 * 1024),
-        cost_estimate=pl.CostEstimate(flops=8_000_000_000, bytes_accessed=4_000_000, transcendentals=0),
-        name="project",
-    )(combined, labels, inverse)
-    prolong = projected.reshape(tests.shape)
-    return prolong, received.reshape(1, slots_total, K * K)
+        name="widen",
+    )(received, projected)
+    return prolong.reshape(tests.shape), basis
 
 
 def solution(mesh):

time: 101 us -> 86.8 us (0.86)
  Pallas kernels: 68.1 us -> 83.6 us
  starting transfers between devices: 13.5 us -> 0 us
  waiting for transfers between devices: 9.63 us -> 0 us
  local copies, waits for them, and re-layouts: 7.1 us -> 2.38 us
  other arithmetic: 1.6 us -> 0 us
    pallas_call x1 -> x2, Pallas kernels: 9.66 us -> 25.3 us  [the longest x1 22.6 us: shards(): pl.pallas_call(functools.partial(project_kernel, n_wide, n_narrow), out_s...]
    all_to_all x1 -> x0, starting transfers between devices: 13.5 us -> none  [shards(): lax.all_to_all(packed.reshape(n_wide * n_narrow, SLOT, K * K), ('wide', '...]
    all_to_all x1 -> x0, waiting for transfers between devices: 9.63 us -> none  [shards(): lax.all_to_all(packed.reshape(n_wide * n_narrow, SLOT, K * K), ('wide', '...]
    reshape x4 -> x0, local copies, waits for them, and re-layouts: 5.24 us -> none  [the longest x1 1.69 us: shards(): return (prolong, received.reshape(1, slots_total, K * K))]
    unnamed x7 -> x8, local copies, waits for them, and re-layouts: 1.77 us -> 2.38 us
  transfers between devices with their start and end apart: 1 -> 0, of which waited for: 1 -> 0; matrix products, arithmetic and copies ran while one was open for 0% -> 0% of each run, Pallas kernels for 10% -> 0%
where the time goes in v3:
time: 86.8 us; the launch traced here: 86.6 us
  Pallas kernels  83.6 us (96%)
  local copies, waits for them, and re-layouts  2.38 us (3%)
    pallas_call x1, Pallas kernels, shards(): pl.pallas_call(functools.partial(relax_kernel, n_wide), out_shape=(jax.Sh...  56.6 us
    pallas_call x1, Pallas kernels, shards(): pl.pallas_call(functools.partial(project_kernel, n_wide, n_narrow), out_s...  22.6 us
    pallas_call x1, Pallas kernels, shards(): pl.pallas_call(widen_kernel, out_shape=(jax.ShapeDtypeStruct((1, slots_to...  2.69 us
    unnamed x8, local copies, waits for them, and re-layouts  2.38 us

profile of v3, /device:TPU:1, one launch (start us, length us, event | category | flops | bytes accessed | tf_op | source)
XLA Modules:
  0.0 86.6 jit_solution(7048820929978900137)
XLA Ops:
  0.6 0.0 copy-start.3
  0.6 0.0 copy-start.2
  0.7 56.6 %relax_far_gram.1 = (f32[16,96,256]{2,1,0:T(8,128)}, f32[656,128]{1,0:T(8,128)}) custom-call(f32[16,384,64]{2,1,0:T(8,128)} %bitcast.13, f32[576,64]{1,0:T(8,128)} %bitcast.14, f32[384,64]{1,0:T(8,128)} %bitcast.15, f32[3,3,6]{2,1,0:T(4,128)} %bitcast.16, bf16[16,3,256,256]{3,2,1,0:T(8,128)(2,1)} %bitcast.12, s32[3,1,16]{2,1,0:T(1,128)} %bitcast.17, ...), custom_call_target="tpu_custom_call" | custom-call | tf_op jit(solution)/shard_map/relax_far_gram/pallas_call | solution.py:471
  57.3 0.0 copy-done.3
  57.3 0.0 copy-start.1
  57.3 1.0 %copy-done.1 = f32[656,128]{1,0:T(8,128)S(1)} copy-done((f32[656,128]{1,0:T(8,128)S(1)}, f32[656,128]{1,0:T(8,128)}, u32[]{:S(2)}) %copy-start.1) | copy-done | bytes 335896
  58.3 1.6 %factor.1 = (f32[256,640]{1,0:T(8,128)S(1)}, bf16[640,384]{1,0:T(8,128)(2,1)S(1)}) custom-call(f32[656,128]{1,0:T(8,128)S(1)} %copy-done.1, s32[1,64]{1,0:T(1,128)S(1)} %bitcast.11), custom_call_target="tpu_custom_call" | custom-call | tf_op jit(solution)/shard_map/factor/pallas_call | solution.py:521
  59.9 0.0 copy-done.2
  59.9 0.0 copy-start
  59.9 1.4 %copy-done = f32[16,96,256]{2,1,0:T(8,128)S(1)} copy-done((f32[16,96,256]{2,1,0:T(8,128)S(1)}, f32[16,96,256]{2,1,0:T(8,128)}, u32[]{:S(2)}) %copy-start) | copy-done | bytes 1572888
  61.3 22.6 %project.1 = (f32[16,384,64]{2,1,0:T(8,128)S(1)}, f32[256,640]{1,0:T(8,128)S(1)}) custom-call(f32[256,640]{1,0:T(8,128)S(1)} %get-tuple-element.11.packed_ref, f32[16,96,256]{2,1,0:T(8,128)S(1)} %copy-done, s32[64,64]{1,0:T(8,128)S(1)} %bitcast.10, bf16[640,384]{1,0:T(8,128)(2,1)S(1)} %get-tuple-element.13.inverse_ref), custom_call_target="tpu_custom_call" | custom-call | tf_op jit(solution)/shard_map/project/pallas_call | solution.py:534
  83.9 2.7 %widen.1 = (f32[1,256,1024]{2,1,0:T(8,128)}, f32[16,384,64]{2,1,0:T(8,128)}) custom-call(f32[256,640]{1,0:T(8,128)S(1)} %get-tuple-element.14.received_ref, f32[16,384,64]{2,1,0:T(8,128)S(1)} %get-tuple-element.15.prolong_in), custom_call_target="tpu_custom_call" | custom-call | tf_op jit(solution)/shard_map/widen/pallas_call | solution.py:555
Async XLA Ops:
  0.6 56.7 %copy-start.3 = (s32[64]{0:T(128)S(1)}, s32[64]{0:T(128)}, u32[]{:S(2)}) copy-start(s32[64]{0:T(128)} %param.15) | copy-start | bytes 772
  0.6 59.3 %copy-start.2 = (s32[16,4,64]{2,1,0:T(4,128)S(1)}, s32[16,4,64]{2,1,0:T(4,128)}, u32[]{:S(2)}) copy-start(s32[16,4,64]{2,1,0:T(4,128)} %param.14) | copy-start | bytes 49156
  57.3 1.0 %copy-start.1 = (f32[656,128]{1,0:T(8,128)S(1)}, f32[656,128]{1,0:T(8,128)}, u32[]{:S(2)}) copy-start(f32[656,128]{1,0:T(8,128)} %get-tuple-element.10.gram_ref) | copy-start | bytes 1007620
  59.9 1.4 %copy-start = (f32[16,96,256]{2,1,0:T(8,128)S(1)}, f32[16,96,256]{2,1,0:T(8,128)}, u32[]{:S(2)}) copy-start(f32[16,96,256]{2,1,0:T(8,128)} %get-tuple-element.12.comb_ref) | copy-start | bytes 4718596

commit v4 on v3

--- a/solution.py
+++ b/solution.py
@@ -23,8 +23,10 @@
 for place, (block_k, block_b) in enumerate(BLOCKS):
     STARTS.setdefault(block_k, 8 * place)
 GRAM_ROWS = TRI + 16
-CHUNKS = 4
+CHUNKS = 8
 PART = PLANES // CHUNKS
+GRAM_PARTS = 4
+EARLY = 4
 
 
 def split3(x):
@@ -56,12 +58,12 @@
 
     def plane_at(i):
         half = i // 2
-        return jnp.where(lax.rem(i, 2) == 0, half, PLANES - 1 - half)
+        return jnp.where(lax.rem(i, 2) == 0, PLANES // 2 - 1 - half, PLANES // 2 + half)
 
     tests_copies = []
     for q in range(CHUNKS):
-        for j, start in enumerate((2 * q, PLANES - 2 - 2 * q)):
-            span = pl.ds(start, 2)
+        for j, start in enumerate((PLANES // 2 - 1 - q, PLANES // 2 + q)):
+            span = pl.ds(start, 1)
             copy = pltpu.make_async_copy(tests_hbm.at[span], raw.at[span], tests_sems.at[2 * q + j])
             copy.start()
             tests_copies.append(copy)
@@ -102,9 +104,30 @@
         )
         return up, down
 
+    has_right = w < n_wide - 1
+    has_left = w > 0
+
     def start_x(s):
-        for copy in x_copies(s):
-            copy.start()
+        up, down = x_copies(s)
+        pl.when(has_right)(up.start)
+        pl.when(has_left)(down.start)
+
+    def wait_x(s):
+        up, down = x_copies(s)
+        pl.when(has_right)(up.wait_send)
+        pl.when(has_left)(up.wait_recv)
+        pl.when(has_left)(down.wait_send)
+        pl.when(has_right)(down.wait_recv)
+
+    @pl.when(jnp.logical_not(has_left))
+    def clear_left():
+        for field in fields:
+            field[0] = jnp.zeros((ROWS, NODES), jnp.float32)
+
+    @pl.when(jnp.logical_not(has_right))
+    def clear_right():
+        for field in fields:
+            field[PLANES + 1] = jnp.zeros((ROWS, NODES), jnp.float32)
 
     def unpack_tests(i, carry):
         p = plane_at(i)
@@ -121,8 +144,8 @@
         lax.fori_loop(q * PART, (q + 1) * PART, unpack_tests, 0)
         if q == 0:
             pl.semaphore_wait(barrier, 3)
-            start_x(0)
         y_copy(0, q).start()
+    start_x(0)
 
     lane_wide = lax.broadcasted_iota(jnp.int32, (8, NODES), 1)
     z_place = lax.rem(lane_wide, 64)
@@ -196,8 +219,8 @@
 
     def plane_copies(q):
         copies = []
-        for j, start in enumerate((2 * q, PLANES - 2 - 2 * q)):
-            span = pl.ds(start, 2)
+        for j, start in enumerate((PLANES // 2 - 1 - q, PLANES // 2 + q)):
+            span = pl.ds(start, 1)
             for side, (target, landing) in enumerate(((right, from_left), (left, from_right))):
                 at = 4 * q + 2 * j + side
                 copies.append(
@@ -209,16 +232,13 @@
         return copies
 
     for s in range(SWEEPS):
-        for copy in x_copies(s):
-            copy.wait()
 
         def one_chunk(q, carry, s=s):
             y_copy(s, q).wait()
+            pl.when(q == CHUNKS - 1)(lambda: wait_x(s))
 
             def one_plane(j, inner):
                 sweep_plane(s, q * PART + j)
-                if s + 1 < SWEEPS:
-                    pl.when(jnp.logical_and(q == 0, j == 1))(lambda: start_x(s + 1))
                 return inner
 
             lax.fori_loop(0, PART, one_plane, 0)
@@ -230,6 +250,8 @@
             return carry
 
         lax.fori_loop(0, CHUNKS, one_chunk, 0)
+        if s + 1 < SWEEPS:
+            start_x(s + 1)
 
     tiles_copy.wait()
     sources = [from_left, planes, from_right]
@@ -256,11 +278,11 @@
 
     lax.fori_loop(0, PLANES, side_far, 0)
 
-    pairs = len(BLOCKS) // 2 // CHUNKS
+    pairs = len(BLOCKS) // 2 // GRAM_PARTS
     rows_part = 16 * pairs
 
     def gram_copy(t):
-        height = rows_part if t + 1 < CHUNKS else GRAM_ROWS - rows_part * t
+        height = rows_part if t + 1 < GRAM_PARTS else GRAM_ROWS - rows_part * t
         span = pl.ds(rows_part * t, height)
         return pltpu.make_async_remote_copy(
             src_ref=acc.at[span], dst_ref=gram_in.at[span], send_sem=gsend_sems.at[t], recv_sem=grecv_sems.at[t],
@@ -270,7 +292,7 @@
     def contract(values, member):
         return lax.dot_general(values, member, (((1,), (1,)), ((), ())), preferred_element_type=jnp.float32)
 
-    for t in range(CHUNKS):
+    for t in range(GRAM_PARTS):
 
         def gram_planes(h, carry, t=t):
             for side in range(2):
@@ -294,7 +316,7 @@
                     term = contract(outer[piece, :, lanes], member)
                     total = term if total is None else total + term
             acc[pl.ds(rows_part * t, rows_part), :] += total
-            if t + 1 == CHUNKS:
+            if t + 1 == GRAM_PARTS:
                 ones = jnp.ones((16, NODES), jnp.bfloat16)
                 acc[TRI:GRAM_ROWS] += contract(ones, members[2 * h]) + contract(ones, members[2 * h + 1])
             return carry
@@ -302,7 +324,7 @@
         lax.fori_loop(0, PLANES // 2, gram_planes, 0)
         gram_copy(t).start()
 
-    for t in range(CHUNKS):
+    for t in range(GRAM_PARTS):
         gram_copy(t).wait()
     gram_ref[...] = acc[...] + gram_in[...]
 
@@ -408,7 +430,7 @@
                     out_ref[r, pl.ds(96 * b + 4 * c + y, 8, stride=12), :] = totals[c][:, 64 * y : 64 * (y + 1)]
         return carry
 
-    lax.fori_loop(0, PART, project_plane, 0)
+    lax.fori_loop(0, EARLY, project_plane, 0)
     pl.semaphore_wait(barrier, count - 1)
 
     def send(i, carry):
@@ -420,7 +442,7 @@
         return carry
 
     lax.fori_loop(1, count, send, 0)
-    lax.fori_loop(PART, PLANES, project_plane, 0)
+    lax.fori_loop(EARLY, PLANES, project_plane, 0)
     everything = pltpu.make_async_remote_copy(
         src_ref=packed_ref, dst_ref=landing, send_sem=send_sem, recv_sem=recv_sem, device_id=peer(1)[1],
         device_id_type=MESH,
@@ -490,7 +512,7 @@
             vmem((PLANES, ROWS, NODES), bf16),
             vmem((PLANES, 3, NODES, NODES), bf16),
             vmem((PLANES, WIDTH, NODES), bf16),
-            vmem((3, TRI // CHUNKS, 2 * NODES), bf16),
+            vmem((3, TRI // GRAM_PARTS, 2 * NODES), bf16),
             vmem((GRAM_ROWS, WIDTH)),
             vmem((GRAM_ROWS, WIDTH)),
             pltpu.SemaphoreType.DMA((2 * CHUNKS,)),
@@ -501,8 +523,8 @@
             pltpu.SemaphoreType.DMA((SWEEPS * CHUNKS,)),
             pltpu.SemaphoreType.DMA((4 * CHUNKS,)),
             pltpu.SemaphoreType.DMA((4 * CHUNKS,)),
-            pltpu.SemaphoreType.DMA((CHUNKS,)),
-            pltpu.SemaphoreType.DMA((CHUNKS,)),
+            pltpu.SemaphoreType.DMA((GRAM_PARTS,)),
+            pltpu.SemaphoreType.DMA((GRAM_PARTS,)),
         ],
         compiler_params=pltpu.CompilerParams(
             collective_id=0, has_side_effects=True, vmem_limit_bytes=56 * 1024 * 1024

time: 86.8 us -> 87.7 us (1.010)
    pallas_call x1, Pallas kernels: 56.6 us -> 58 us  [shards(): pl.pallas_call(functools.partial(relax_kernel, n_wide), out_shape=(jax.Sh...]
where the time goes in v4:
time: 87.7 us; the launch traced here: 87.5 us
  Pallas kernels  84.4 us (96%)
  local copies, waits for them, and re-layouts  2.38 us (3%)
    pallas_call x1, Pallas kernels, shards(): pl.pallas_call(functools.partial(relax_kernel, n_wide), out_shape=(jax.Sh...  58 us
    pallas_call x1, Pallas kernels, shards(): pl.pallas_call(functools.partial(project_kernel, n_wide, n_narrow), out_s...  22.1 us
    pallas_call x1, Pallas kernels, shards(): pl.pallas_call(widen_kernel, out_shape=(jax.ShapeDtypeStruct((1, slots_to...  2.69 us
    unnamed x8, local copies, waits for them, and re-layouts  2.38 us

profile of v4, /device:TPU:1, one launch (start us, length us, event | category | flops | bytes accessed | tf_op | source)
XLA Modules:
  0.0 87.5 jit_solution(5244427257751315723)
XLA Ops:
  0.6 0.0 copy-start.3
  0.6 0.0 copy-start.2
  0.7 58.0 %relax_far_gram.1 = (f32[16,96,256]{2,1,0:T(8,128)}, f32[656,128]{1,0:T(8,128)}) custom-call(f32[16,384,64]{2,1,0:T(8,128)} %bitcast.13, f32[576,64]{1,0:T(8,128)} %bitcast.14, f32[384,64]{1,0:T(8,128)} %bitcast.15, f32[3,3,6]{2,1,0:T(4,128)} %bitcast.16, bf16[16,3,256,256]{3,2,1,0:T(8,128)(2,1)} %bitcast.12, s32[3,1,16]{2,1,0:T(1,128)} %bitcast.17, ...), custom_call_target="tpu_custom_call" | custom-call | tf_op jit(solution)/shard_map/relax_far_gram/pallas_call | solution.py:493
  58.7 0.0 copy-done.3
  58.7 0.0 copy-start.1
  58.7 1.0 %copy-done.1 = f32[656,128]{1,0:T(8,128)S(1)} copy-done((f32[656,128]{1,0:T(8,128)S(1)}, f32[656,128]{1,0:T(8,128)}, u32[]{:S(2)}) %copy-start.1) | copy-done | bytes 335896
  59.6 1.6 %factor.1 = (f32[256,640]{1,0:T(8,128)S(1)}, bf16[640,384]{1,0:T(8,128)(2,1)S(1)}) custom-call(f32[656,128]{1,0:T(8,128)S(1)} %copy-done.1, s32[1,64]{1,0:T(1,128)S(1)} %bitcast.11), custom_call_target="tpu_custom_call" | custom-call | tf_op jit(solution)/shard_map/factor/pallas_call | solution.py:543
  61.3 0.0 copy-done.2
  61.3 0.0 copy-start
  61.3 1.4 %copy-done = f32[16,96,256]{2,1,0:T(8,128)S(1)} copy-done((f32[16,96,256]{2,1,0:T(8,128)S(1)}, f32[16,96,256]{2,1,0:T(8,128)}, u32[]{:S(2)}) %copy-start) | copy-done | bytes 1572888
  62.7 22.1 %project.1 = (f32[16,384,64]{2,1,0:T(8,128)S(1)}, f32[256,640]{1,0:T(8,128)S(1)}) custom-call(f32[256,640]{1,0:T(8,128)S(1)} %get-tuple-element.11.packed_ref, f32[16,96,256]{2,1,0:T(8,128)S(1)} %copy-done, s32[64,64]{1,0:T(8,128)S(1)} %bitcast.10, bf16[640,384]{1,0:T(8,128)(2,1)S(1)} %get-tuple-element.13.inverse_ref), custom_call_target="tpu_custom_call" | custom-call | tf_op jit(solution)/shard_map/project/pallas_call | solution.py:556
  84.8 2.7 %widen.1 = (f32[1,256,1024]{2,1,0:T(8,128)}, f32[16,384,64]{2,1,0:T(8,128)}) custom-call(f32[256,640]{1,0:T(8,128)S(1)} %get-tuple-element.14.received_ref, f32[16,384,64]{2,1,0:T(8,128)S(1)} %get-tuple-element.15.prolong_in), custom_call_target="tpu_custom_call" | custom-call | tf_op jit(solution)/shard_map/widen/pallas_call | solution.py:577
Async XLA Ops:
  0.6 58.0 %copy-start.3 = (s32[64]{0:T(128)S(1)}, s32[64]{0:T(128)}, u32[]{:S(2)}) copy-start(s32[64]{0:T(128)} %param.15) | copy-start | bytes 772
  0.6 60.6 %copy-start.2 = (s32[16,4,64]{2,1,0:T(4,128)S(1)}, s32[16,4,64]{2,1,0:T(4,128)}, u32[]{:S(2)}) copy-start(s32[16,4,64]{2,1,0:T(4,128)} %param.14) | copy-start | bytes 49156
  58.7 1.0 %copy-start.1 = (f32[656,128]{1,0:T(8,128)S(1)}, f32[656,128]{1,0:T(8,128)}, u32[]{:S(2)}) copy-start(f32[656,128]{1,0:T(8,128)} %get-tuple-element.10.gram_ref) | copy-start | bytes 1007620
  61.3 1.4 %copy-start = (f32[16,96,256]{2,1,0:T(8,128)S(1)}, f32[16,96,256]{2,1,0:T(8,128)}, u32[]{:S(2)}) copy-start(f32[16,96,256]{2,1,0:T(8,128)} %get-tuple-element.12.comb_ref) | copy-start | bytes 4718596

commit v5 on v4

--- a/solution.py
+++ b/solution.py
@@ -41,13 +41,14 @@
     return jnp.concatenate(rows, axis=1)
 
 
-def relax_kernel(
-    n_wide,
-    tests_hbm, bi_ref, fw_ref, mix_ref, tiles_hbm, col_ref, label_ref,
-    comb_ref, gram_ref,
+def setup_kernel(
+    n_wide, n_narrow,
+    tests_hbm, bi_ref, fw_ref, mix_ref, tiles_hbm, col_ref, label_ref, owner_ref,
+    out_ref, received_ref,
+    comb_ref, lower, inv, inverse_ref, packed_ref, landing, look, spare,
     raw, x0, x1, x2, coef, ysend, yrecv, ydup, from_left, planes, from_right, tiles, members, outer, acc, gram_in,
     tests_sems, tiles_sem, xsend_sems, xrecv_sems, ysend_sems, yrecv_sems, psend_sems, precv_sems, gsend_sems,
-    grecv_sems,
+    grecv_sems, send_sem, recv_sem,
 ):
     w = lax.axis_index("wide")
     n = lax.axis_index("narrow")
@@ -71,8 +72,18 @@
     tiles_copy.start()
 
     barrier = pltpu.get_barrier_semaphore()
-    for target in ((left, n), (right, n), (w, other)):
-        pl.semaphore_signal(barrier, inc=1, device_id=target, device_id_type=MESH)
+    count = n_wide * n_narrow
+    me = w * n_narrow + n
+
+    def peer(i):
+        index = lax.rem(me + i, count)
+        return index, (index // n_narrow, lax.rem(index, n_narrow))
+
+    def greet(i, carry):
+        pl.semaphore_signal(barrier, inc=1, device_id=peer(i)[1], device_id_type=MESH)
+        return carry
+
+    lax.fori_loop(1, count, greet, 0)
 
     lane = lax.broadcasted_iota(jnp.int32, (K + 16, WIDTH), 1)
     low_half = lane < 64
@@ -142,10 +153,6 @@
         tests_copies[2 * q].wait()
         tests_copies[2 * q + 1].wait()
         lax.fori_loop(q * PART, (q + 1) * PART, unpack_tests, 0)
-        if q == 0:
-            pl.semaphore_wait(barrier, 3)
-        y_copy(0, q).start()
-    start_x(0)
 
     lane_wide = lax.broadcasted_iota(jnp.int32, (8, NODES), 1)
     z_place = lax.rem(lane_wide, 64)
@@ -177,7 +184,12 @@
         members[p] = jnp.where(groups == label, 1.0, 0.0).astype(jnp.bfloat16)
         return carry
 
-    lax.fori_loop(0, PLANES, make_coef, 0)
+    lax.fori_loop(0, EARLY, make_coef, 0)
+    pl.semaphore_wait(barrier, count - 1)
+    for q in range(CHUNKS):
+        y_copy(0, q).start()
+    start_x(0)
+    lax.fori_loop(EARLY, PLANES, make_coef, 0)
 
     def sweep_plane(s, i):
         p = plane_at(i)
@@ -326,7 +338,52 @@
 
     for t in range(GRAM_PARTS):
         gram_copy(t).wait()
-    gram_ref[...] = acc[...] + gram_in[...]
+
+    def gram_rows(first, height):
+        span = pl.ds(first, height)
+        return acc[span, :] + gram_in[span, :]
+
+    factorize(gram_rows, owner_ref, packed_ref, inverse_ref, lower, inv)
+
+    own_span = pl.ds(SLOT * me, SLOT)
+    pltpu.make_async_copy(packed_ref.at[own_span], landing.at[own_span], recv_sem).start()
+    pltpu.make_async_copy(packed_ref.at[own_span], spare, send_sem).start()
+
+    def send(i, carry):
+        index, device = peer(i)
+        pltpu.make_async_remote_copy(
+            src_ref=packed_ref.at[pl.ds(SLOT * index, SLOT)], dst_ref=landing.at[own_span], send_sem=send_sem,
+            recv_sem=recv_sem, device_id=device, device_id_type=MESH,
+        ).start()
+        return carry
+
+    lax.fori_loop(1, count, send, 0)
+
+    def project_plane(r, carry):
+        member = members[r]
+        look[...] = jnp.dot(
+            inverse_ref[...], jnp.concatenate([member, member, member], axis=0), preferred_element_type=jnp.float32
+        )
+        for b in range(K // 8):
+            totals = [None] * 3
+            for l in range(8 * (b + 1)):
+                weight = look[pl.ds(STARTS[l] + 8 * (b - l // 8), 8), :]
+                for c in range(3):
+                    term = weight * comb_ref[r, c * K + l : c * K + l + 1, :]
+                    totals[c] = term if totals[c] is None else totals[c] + term
+            for c in range(3):
+                for y in range(4):
+                    out_ref[r, pl.ds(96 * b + 4 * c + y, 8, stride=12), :] = totals[c][:, 64 * y : 64 * (y + 1)]
+        return carry
+
+    lax.fori_loop(0, PLANES, project_plane, 0)
+    everything = pltpu.make_async_remote_copy(
+        src_ref=packed_ref, dst_ref=landing, send_sem=send_sem, recv_sem=recv_sem, device_id=peer(1)[1],
+        device_id_type=MESH,
+    )
+    everything.wait_send()
+    everything.wait_recv()
+    received_ref[...] = landing[...]
 
 
 def slot_table(owner_ref, slots_total):
@@ -345,14 +402,14 @@
     return jnp.where(slots == lanes, 1.0, 0.0).astype(jnp.bfloat16)
 
 
-def factor_kernel(gram_ref, owner_ref, packed_ref, inverse_ref, lower, inv):
-    scale = 1.0 / (3.0 * gram_ref[TRI : TRI + 1, :])
+def factorize(gram_rows, owner_ref, packed_ref, inverse_ref, lower, inv):
+    scale = 1.0 / (3.0 * gram_rows(TRI, 1))
     row = lax.broadcasted_iota(jnp.int32, (K, WIDTH), 0)
     columns = []
     for k in range(K):
         first = 8 * (k // 8)
         height = K - first
-        column = gram_ref[pl.ds(STARTS[k], height), :] * scale
+        column = gram_rows(STARTS[k], height) * scale
         columns.append(column + jnp.where(row[first:] == k, RIDGE, 0.0))
     reciprocals = []
     for k in range(K):
@@ -387,71 +444,6 @@
     packed_ref[...] = total
 
 
-def project_kernel(
-    n_wide, n_narrow, packed_ref, comb_ref, label_ref, inverse_ref, out_ref, received_ref, landing, look, spare,
-    send_sem, recv_sem,
-):
-    count = n_wide * n_narrow
-    w = lax.axis_index("wide")
-    n = lax.axis_index("narrow")
-    me = w * n_narrow + n
-    barrier = pltpu.get_barrier_semaphore()
-
-    def peer(i):
-        index = lax.rem(me + i, count)
-        return index, (index // n_narrow, lax.rem(index, n_narrow))
-
-    def greet(i, carry):
-        pl.semaphore_signal(barrier, inc=1, device_id=peer(i)[1], device_id_type=MESH)
-        return carry
-
-    lax.fori_loop(1, count, greet, 0)
-    own_span = pl.ds(SLOT * me, SLOT)
-    pltpu.make_async_copy(packed_ref.at[own_span], landing.at[own_span], recv_sem).start()
-    pltpu.make_async_copy(packed_ref.at[own_span], spare, send_sem).start()
-
-    groups = lax.broadcasted_iota(jnp.int32, (WIDTH, NODES), 0)
-
-    def project_plane(r, carry):
-        label = join_rows([label_ref[pl.ds(4 * r + y, 1), :] for y in range(4)])
-        member = jnp.where(groups == label, 1.0, 0.0).astype(jnp.bfloat16)
-        look[...] = jnp.dot(
-            inverse_ref[...], jnp.concatenate([member, member, member], axis=0), preferred_element_type=jnp.float32
-        )
-        for b in range(K // 8):
-            totals = [None] * 3
-            for l in range(8 * (b + 1)):
-                weight = look[pl.ds(STARTS[l] + 8 * (b - l // 8), 8), :]
-                for c in range(3):
-                    term = weight * comb_ref[r, c * K + l : c * K + l + 1, :]
-                    totals[c] = term if totals[c] is None else totals[c] + term
-            for c in range(3):
-                for y in range(4):
-                    out_ref[r, pl.ds(96 * b + 4 * c + y, 8, stride=12), :] = totals[c][:, 64 * y : 64 * (y + 1)]
-        return carry
-
-    lax.fori_loop(0, EARLY, project_plane, 0)
-    pl.semaphore_wait(barrier, count - 1)
-
-    def send(i, carry):
-        index, device = peer(i)
-        pltpu.make_async_remote_copy(
-            src_ref=packed_ref.at[pl.ds(SLOT * index, SLOT)], dst_ref=landing.at[own_span], send_sem=send_sem,
-            recv_sem=recv_sem, device_id=device, device_id_type=MESH,
-        ).start()
-        return carry
-
-    lax.fori_loop(1, count, send, 0)
-    lax.fori_loop(EARLY, PLANES, project_plane, 0)
-    everything = pltpu.make_async_remote_copy(
-        src_ref=packed_ref, dst_ref=landing, send_sem=send_sem, recv_sem=recv_sem, device_id=peer(1)[1],
-        device_id_type=MESH,
-    )
-    everything.wait_send()
-    everything.wait_recv()
-    received_ref[...] = landing[...]
-
-
 def widen_kernel(received_ref, prolong_in, basis_ref, prolong_out, sem):
     copy = pltpu.make_async_copy(prolong_in, prolong_out, sem)
     copy.start()
@@ -486,19 +478,28 @@
     bf16 = jnp.bfloat16
     whole = pl.BlockSpec(memory_space=pltpu.VMEM)
     any_spec = pl.BlockSpec(memory_space=pl.ANY)
+    hbm = pl.BlockSpec(memory_space=pltpu.HBM)
     smem = pl.BlockSpec(memory_space=pltpu.SMEM)
     labels = aggregate.reshape(PLANES * 4, 64)
 
     slots_total = n_wide * n_narrow * SLOT
-    combined, gram = pl.pallas_call(
-        functools.partial(relax_kernel, n_wide),
+    projected, received = pl.pallas_call(
+        functools.partial(setup_kernel, n_wide, n_narrow),
         out_shape=(
-            jax.ShapeDtypeStruct((PLANES, ROWS, NODES), jnp.float32),
-            jax.ShapeDtypeStruct((GRAM_ROWS, WIDTH), jnp.float32),
+            jax.ShapeDtypeStruct((PLANES, 4 * ROWS, 64), jnp.float32),
+            jax.ShapeDtypeStruct((slots_total, TRI), jnp.float32),
         ),
-        in_specs=[any_spec, whole, whole, smem, any_spec, smem, whole],
+        in_specs=[hbm, whole, whole, smem, hbm, smem, whole, whole],
         out_specs=(whole, whole),
         scratch_shapes=[
+            vmem((PLANES, ROWS, NODES)),
+            vmem((TRI, WIDTH)),
+            vmem((TRI, WIDTH)),
+            vmem((TRI, 3 * WIDTH), bf16),
+            vmem((slots_total, TRI)),
+            vmem((slots_total, TRI)),
+            vmem((TRI, NODES)),
+            vmem((SLOT, TRI)),
             vmem((PLANES, 4 * ROWS, 64)),
             vmem((PLANES + 2, ROWS, NODES)),
             vmem((PLANES + 2, ROWS, NODES)),
@@ -525,11 +526,13 @@
             pltpu.SemaphoreType.DMA((4 * CHUNKS,)),
             pltpu.SemaphoreType.DMA((GRAM_PARTS,)),
             pltpu.SemaphoreType.DMA((GRAM_PARTS,)),
+            pltpu.SemaphoreType.DMA,
+            pltpu.SemaphoreType.DMA,
         ],
         compiler_params=pltpu.CompilerParams(
-            collective_id=0, has_side_effects=True, vmem_limit_bytes=56 * 1024 * 1024
+            collective_id=0, has_side_effects=True, vmem_limit_bytes=48 * 1024 * 1024
         ),
-        name="relax_far_gram",
+        name="setup",
     )(
         tests.reshape(PLANES, 4 * ROWS, 64),
         block_inverse.reshape(PLANES * 36, 64),
@@ -538,41 +541,8 @@
         far_tiles.reshape(PLANES, 3, NODES, NODES),
         far_column.transpose(2, 1, 0),
         labels,
+        owner_map.reshape(1, owner_map.shape[0]),
     )
-
-    packed, inverse = pl.pallas_call(
-        factor_kernel,
-        out_shape=(
-            jax.ShapeDtypeStruct((slots_total, TRI), jnp.float32),
-            jax.ShapeDtypeStruct((TRI, 3 * WIDTH), bf16),
-        ),
-        in_specs=[whole, whole],
-        out_specs=(whole, whole),
-        scratch_shapes=[vmem((TRI, WIDTH)), vmem((TRI, WIDTH))],
-        compiler_params=pltpu.CompilerParams(vmem_limit_bytes=32 * 1024 * 1024),
-        name="factor",
-    )(gram, owner_map.reshape(1, owner_map.shape[0]))
-
-    projected, received = pl.pallas_call(
-        functools.partial(project_kernel, n_wide, n_narrow),
-        out_shape=(
-            jax.ShapeDtypeStruct((PLANES, 4 * ROWS, 64), jnp.float32),
-            jax.ShapeDtypeStruct((slots_total, TRI), jnp.float32),
-        ),
-        in_specs=[whole, whole, whole, whole],
-        out_specs=(whole, whole),
-        scratch_shapes=[
-            vmem((slots_total, TRI)),
-            vmem((TRI, NODES)),
-            vmem((SLOT, TRI)),
-            pltpu.SemaphoreType.DMA,
-            pltpu.SemaphoreType.DMA,
-        ],
-        compiler_params=pltpu.CompilerParams(
-            collective_id=1, has_side_effects=True, vmem_limit_bytes=40 * 1024 * 1024
-        ),
-        name="project",
-    )(packed, combined, labels, inverse)
 
     basis, prolong = pl.pallas_call(
         widen_kernel,

time: 87.7 us -> 85.2 us (0.971)
  the two profiles are of different devices: /device:TPU:1 before, /device:TPU:2 now
where the time goes in v5:
time: 85.2 us; the launch traced here: 84.9 us
  Pallas kernels  79.5 us (93%)
  local copies, waits for them, and re-layouts  4.66 us (5%)
    pallas_call x1, Pallas kernels, shards(): pl.pallas_call(functools.partial(setup_kernel, n_wide, n_narrow), out_sha...  76.9 us
    unnamed x12, local copies, waits for them, and re-layouts  4.66 us
    pallas_call x1, Pallas kernels, shards(): pl.pallas_call(widen_kernel, out_shape=(jax.ShapeDtypeStruct((1, slots_to...  2.69 us

profile of v5, /device:TPU:2, one launch (start us, length us, event | category | flops | bytes accessed | tf_op | source)
XLA Modules:
  0.0 84.9 jit_solution(6560351830131657028)
XLA Ops:
  0.6 0.0 copy-start
  0.6 1.0 %copy-done = f32[16,3,3,4,64]{4,3,2,1,0:T(4,128)S(1)} copy-done((f32[16,3,3,4,64]{4,3,2,1,0:T(4,128)S(1)}, f32[16,3,3,4,64]{4,3,2,1,0:T(4,128)}, u32[]{:S(2)}) %copy-start) | copy-done | bytes 147480
  1.6 0.0 copy-start.1
  1.6 0.9 %copy-done.1 = f32[16,6,4,64]{3,2,1,0:T(4,128)S(1)} copy-done((f32[16,6,4,64]{3,2,1,0:T(4,128)S(1)}, f32[16,6,4,64]{3,2,1,0:T(4,128)}, u32[]{:S(2)}) %copy-start.1) | copy-done | bytes 98328
  2.5 0.0 copy-start.2
  2.5 0.8 copy-done.2
  3.3 0.0 copy-start.3
  3.3 0.7 copy-done.3
  4.0 0.0 copy-start.4
  4.0 0.7 copy-done.4
  4.7 0.0 copy-start.5
  4.7 0.7 copy-done.5
  5.3 76.9 %setup.1 = (f32[16,384,64]{2,1,0:T(8,128)S(1)}, f32[256,640]{1,0:T(8,128)S(1)}) custom-call(f32[16,384,64]{2,1,0:T(8,128)} %bitcast.16, f32[576,64]{1,0:T(8,128)S(1)} %bitcast.9, f32[384,64]{1,0:T(8,128)S(1)} %bitcast.10, f32[3,3,6]{2,1,0:T(4,128)S(1)} %bitcast.12, bf16[16,3,256,256]{3,2,1,0:T(8,128)(2,1)} %bitcast.15, s32[3,1,16]{2,1,0:T(1,128)S(1)} %bitcast.13, ...), custom_call_target="tpu_custom_call" | custom-call | tf_op jit(solution)/shard_map/setup/pallas_call | solution.py:486
  82.2 2.7 %widen.1 = (f32[1,256,1024]{2,1,0:T(8,128)}, f32[16,384,64]{2,1,0:T(8,128)}) custom-call(f32[256,640]{1,0:T(8,128)S(1)} %get-tuple-element.6.received_ref, f32[16,384,64]{2,1,0:T(8,128)S(1)} %get-tuple-element.7.prolong_in), custom_call_target="tpu_custom_call" | custom-call | tf_op jit(solution)/shard_map/widen/pallas_call | solution.py:547
Async XLA Ops:
  0.6 1.0 %copy-start = (f32[16,3,3,4,64]{4,3,2,1,0:T(4,128)S(1)}, f32[16,3,3,4,64]{4,3,2,1,0:T(4,128)}, u32[]{:S(2)}) copy-start(f32[16,3,3,4,64]{4,3,2,1,0:T(4,128)} %param.9) | copy-start | bytes 442372
  1.6 0.9 %copy-start.1 = (f32[16,6,4,64]{3,2,1,0:T(4,128)S(1)}, f32[16,6,4,64]{3,2,1,0:T(4,128)}, u32[]{:S(2)}) copy-start(f32[16,6,4,64]{3,2,1,0:T(4,128)} %param.10) | copy-start | bytes 294916
  2.5 0.8 copy-start.2
  3.3 0.7 copy-start.3
  4.0 0.7 copy-start.4
  4.7 0.7 copy-start.5

commit v6 on v5

--- a/solution.py
+++ b/solution.py
@@ -27,6 +27,8 @@
 PART = PLANES // CHUNKS
 GRAM_PARTS = 4
 EARLY = 4
+LAG = 5
+PASSES = 4
 
 
 def split3(x):
@@ -44,11 +46,11 @@
 def setup_kernel(
     n_wide, n_narrow,
     tests_hbm, bi_ref, fw_ref, mix_ref, tiles_hbm, col_ref, label_ref, owner_ref,
-    out_ref, received_ref,
+    out_hbm, received_ref,
     comb_ref, lower, inv, inverse_ref, packed_ref, landing, look, spare,
-    raw, x0, x1, x2, coef, ysend, yrecv, ydup, from_left, planes, from_right, tiles, members, outer, acc, gram_in,
+    raw, x0, x1, x2, coef, xsend, xrecv, ysend, yrecv, ydup, from_left, planes, from_right, tiles, members, outer, acc, gram_in,
     tests_sems, tiles_sem, xsend_sems, xrecv_sems, ysend_sems, yrecv_sems, psend_sems, precv_sems, gsend_sems,
-    grecv_sems, send_sem, recv_sem,
+    grecv_sems, send_sem, recv_sem, out_sems,
 ):
     w = lax.axis_index("wide")
     n = lax.axis_index("narrow")
@@ -106,11 +108,11 @@
 
     def x_copies(s):
         up = pltpu.make_async_remote_copy(
-            src_ref=fields[s].at[PLANES], dst_ref=fields[s].at[0], send_sem=xsend_sems.at[2 * s],
+            src_ref=xsend.at[s, 0], dst_ref=xrecv.at[s, 0], send_sem=xsend_sems.at[2 * s],
             recv_sem=xrecv_sems.at[2 * s], device_id=(right, n), device_id_type=MESH,
         )
         down = pltpu.make_async_remote_copy(
-            src_ref=fields[s].at[1], dst_ref=fields[s].at[PLANES + 1], send_sem=xsend_sems.at[2 * s + 1],
+            src_ref=xsend.at[s, 1], dst_ref=xrecv.at[s, 1], send_sem=xsend_sems.at[2 * s + 1],
             recv_sem=xrecv_sems.at[2 * s + 1], device_id=(left, n), device_id_type=MESH,
         )
         return up, down
@@ -120,6 +122,8 @@
 
     def start_x(s):
         up, down = x_copies(s)
+        xsend[s, 0] = fields[s][PLANES].astype(jnp.bfloat16)
+        xsend[s, 1] = fields[s][1].astype(jnp.bfloat16)
         pl.when(has_right)(up.start)
         pl.when(has_left)(down.start)
 
@@ -129,6 +133,15 @@
         pl.when(has_left)(up.wait_recv)
         pl.when(has_left)(down.wait_send)
         pl.when(has_right)(down.wait_recv)
+
+        def widen_left():
+            fields[s][0] = xrecv[s, 0].astype(jnp.float32)
+
+        def widen_right():
+            fields[s][PLANES + 1] = xrecv[s, 1].astype(jnp.float32)
+
+        pl.when(has_left)(widen_left)
+        pl.when(has_right)(widen_right)
 
     @pl.when(jnp.logical_not(has_left))
     def clear_left():
@@ -243,27 +256,29 @@
                 )
         return copies
 
-    for s in range(SWEEPS):
-
-        def one_chunk(q, carry, s=s):
-            y_copy(s, q).wait()
-            pl.when(q == CHUNKS - 1)(lambda: wait_x(s))
-
-            def one_plane(j, inner):
-                sweep_plane(s, q * PART + j)
-                return inner
-
-            lax.fori_loop(0, PART, one_plane, 0)
-            if s + 1 < SWEEPS:
-                y_copy(s + 1, q).start()
-            else:
-                for copy in plane_copies(q):
-                    copy.start()
-            return carry
-
-        lax.fori_loop(0, CHUNKS, one_chunk, 0)
+    def do_chunk(s, q):
+        y_copy(s, q).wait()
+        pl.when(q == CHUNKS - 1)(lambda: wait_x(s))
+
+        def one_plane(j, inner):
+            sweep_plane(s, q * PART + j)
+            return inner
+
+        lax.fori_loop(0, PART, one_plane, 0)
         if s + 1 < SWEEPS:
-            start_x(s + 1)
+            y_copy(s + 1, q).start()
+            pl.when(q == CHUNKS - 1)(lambda: start_x(s + 1))
+        else:
+            for copy in plane_copies(q):
+                copy.start()
+
+    def wave_step(t, carry):
+        for s in range(SWEEPS):
+            q = t - LAG * s
+            pl.when(jnp.logical_and(q >= 0, q < CHUNKS))(functools.partial(do_chunk, s, q))
+        return carry
+
+    lax.fori_loop(0, CHUNKS + LAG * (SWEEPS - 1), wave_step, 0)
 
     tiles_copy.wait()
     sources = [from_left, planes, from_right]
@@ -373,10 +388,22 @@
                     totals[c] = term if totals[c] is None else totals[c] + term
             for c in range(3):
                 for y in range(4):
-                    out_ref[r, pl.ds(96 * b + 4 * c + y, 8, stride=12), :] = totals[c][:, 64 * y : 64 * (y + 1)]
-        return carry
-
-    lax.fori_loop(0, PLANES, project_plane, 0)
+                    raw[r, pl.ds(96 * b + 4 * c + y, 8, stride=12), :] = totals[c][:, 64 * y : 64 * (y + 1)]
+        return carry
+
+    def out_copy(r):
+        return pltpu.make_async_copy(raw.at[r], out_hbm.at[r], out_sems.at[r])
+
+    def project_out(r, carry):
+        project_plane(r, carry)
+        out_copy(r).start()
+        return carry
+
+    def wait_out(r, carry):
+        out_copy(r).wait()
+        return carry
+
+    lax.fori_loop(0, PLANES, project_out, 0)
     everything = pltpu.make_async_remote_copy(
         src_ref=packed_ref, dst_ref=landing, send_sem=send_sem, recv_sem=recv_sem, device_id=peer(1)[1],
         device_id_type=MESH,
@@ -384,6 +411,7 @@
     everything.wait_send()
     everything.wait_recv()
     received_ref[...] = landing[...]
+    lax.fori_loop(0, PLANES, wait_out, 0)
 
 
 def slot_table(owner_ref, slots_total):
@@ -444,11 +472,20 @@
     packed_ref[...] = total
 
 
-def widen_kernel(received_ref, prolong_in, basis_ref, prolong_out, sem):
-    copy = pltpu.make_async_copy(prolong_in, prolong_out, sem)
-    copy.start()
+def widen_kernel(received_ref, prolong_in, basis_ref, prolong_out, passing, in_sems, out_sems):
+    part = PLANES // PASSES
+    inward, outward = [], []
+    for i in range(PASSES):
+        span = pl.ds(part * i, part)
+        inward.append(pltpu.make_async_copy(prolong_in.at[span], passing.at[span], in_sems.at[i]))
+        outward.append(pltpu.make_async_copy(passing.at[span], prolong_out.at[span], out_sems.at[i]))
+    for copy in inward:
+        copy.start()
     pieces = split3(received_ref[...])
     for m in range(K * K // WIDTH):
+        if m >= 2 and m - 2 < PASSES:
+            inward[m - 2].wait()
+            outward[m - 2].start()
         group = m // 2
         width = K - 8 * group
         start = STARTS[8 * group]
@@ -467,7 +504,8 @@
             term = jnp.dot(piece[:, first:last], place, preferred_element_type=jnp.float32)
             total = term if total is None else total + term
         basis_ref[0, :, WIDTH * m : WIDTH * (m + 1)] = total
-    copy.wait()
+    for copy in outward:
+        copy.wait()
 
 
 def vmem(shape, dtype=jnp.float32):
@@ -490,7 +528,7 @@
             jax.ShapeDtypeStruct((slots_total, TRI), jnp.float32),
         ),
         in_specs=[hbm, whole, whole, smem, hbm, smem, whole, whole],
-        out_specs=(whole, whole),
+        out_specs=(any_spec, whole),
         scratch_shapes=[
             vmem((PLANES, ROWS, NODES)),
             vmem((TRI, WIDTH)),
@@ -505,6 +543,8 @@
             vmem((PLANES + 2, ROWS, NODES)),
             vmem((PLANES + 2, ROWS, NODES)),
             vmem((PLANES, 54, 8, NODES)),
+            vmem((SWEEPS, 2, ROWS, NODES), bf16),
+            vmem((SWEEPS, 2, ROWS, NODES), bf16),
             vmem((SWEEPS, PLANES, 48, WIDTH), bf16),
             vmem((SWEEPS, PLANES, 48, WIDTH), bf16),
             vmem((ROWS, WIDTH)),
@@ -528,9 +568,10 @@
             pltpu.SemaphoreType.DMA((GRAM_PARTS,)),
             pltpu.SemaphoreType.DMA,
             pltpu.SemaphoreType.DMA,
+            pltpu.SemaphoreType.DMA((PLANES,)),
         ],
         compiler_params=pltpu.CompilerParams(
-            collective_id=0, has_side_effects=True, vmem_limit_bytes=48 * 1024 * 1024
+            collective_id=0, has_side_effects=True, vmem_limit_bytes=57 * 1024 * 1024
         ),
         name="setup",
     )(
@@ -552,8 +593,12 @@
         ),
         in_specs=[whole, any_spec],
         out_specs=(whole, any_spec),
-        scratch_shapes=[pltpu.SemaphoreType.DMA],
-        compiler_params=pltpu.CompilerParams(vmem_limit_bytes=32 * 1024 * 1024),
+        scratch_shapes=[
+            vmem((PLANES, 4 * ROWS, 64)),
+            pltpu.SemaphoreType.DMA((PASSES,)),
+            pltpu.SemaphoreType.DMA((PASSES,)),
+        ],
+        compiler_params=pltpu.CompilerParams(vmem_limit_bytes=57 * 1024 * 1024),
         name="widen",
     )(received, projected)
     return prolong.reshape(tests.shape), basis

time: 85.2 us -> 82.5 us (0.968)
  the two profiles are of different devices: /device:TPU:2 before, /device:TPU:1 now
where the time goes in v6:
time: 82.5 us; the launch traced here: 82.3 us
  Pallas kernels  81.6 us (99%)
    pallas_call x1, Pallas kernels, shards(): pl.pallas_call(functools.partial(setup_kernel, n_wide, n_narrow), out_sha...  76.7 us
    pallas_call x1, Pallas kernels, shards(): pl.pallas_call(widen_kernel, out_shape=(jax.ShapeDtypeStruct((1, slots_to...  4.93 us

profile of v6, /device:TPU:1, one launch (start us, length us, event | category | flops | bytes accessed | tf_op | source)
XLA Modules:
  0.0 82.3 jit_solution(18195463418571440598)
XLA Ops:
  0.6 76.7 %setup.1 = (f32[16,384,64]{2,1,0:T(8,128)}, f32[256,640]{1,0:T(8,128)}) custom-call(f32[16,384,64]{2,1,0:T(8,128)} %bitcast.10, f32[576,64]{1,0:T(8,128)} %bitcast.11, f32[384,64]{1,0:T(8,128)} %bitcast.12, f32[3,3,6]{2,1,0:T(4,128)} %bitcast.14, bf16[16,3,256,256]{3,2,1,0:T(8,128)(2,1)} %bitcast.9, s32[3,1,16]{2,1,0:T(1,128)} %bitcast.15, ...), custom_call_target="tpu_custom_call" | custom-call | tf_op jit(solution)/shard_map/setup/pallas_call | solution.py:524
  77.3 4.9 %widen.1 = (f32[1,256,1024]{2,1,0:T(8,128)}, f32[16,384,64]{2,1,0:T(8,128)}) custom-call(f32[256,640]{1,0:T(8,128)} %get-tuple-element.6.received_ref, f32[16,384,64]{2,1,0:T(8,128)} %get-tuple-element.7.prolong_in), custom_call_target="tpu_custom_call" | custom-call | tf_op jit(solution)/shard_map/widen/pallas_call | solution.py:588

commit v7 on v6

--- a/solution.py
+++ b/solution.py
@@ -25,9 +25,10 @@
 GRAM_ROWS = TRI + 16
 CHUNKS = 8
 PART = PLANES // CHUNKS
-GRAM_PARTS = 4
+GRAM_PARTS = 1
+SIDES = 4
 EARLY = 4
-LAG = 5
+LAG = 8
 PASSES = 4
 
 
@@ -322,8 +323,8 @@
     for t in range(GRAM_PARTS):
 
         def gram_planes(h, carry, t=t):
-            for side in range(2):
-                r = 2 * h + side
+            for side in range(SIDES):
+                r = SIDES * h + side
                 lanes = pl.ds(side * NODES, NODES)
                 for pair in range(pairs):
                     parts = []
@@ -336,8 +337,8 @@
                     for piece, values in enumerate(split3(jnp.concatenate(parts, axis=0))):
                         outer[piece, pl.ds(16 * pair, 16), lanes] = values
             total = None
-            for side in range(2):
-                member = members[2 * h + side]
+            for side in range(SIDES):
+                member = members[SIDES * h + side]
                 lanes = pl.ds(side * NODES, NODES)
                 for piece in range(3):
                     term = contract(outer[piece, :, lanes], member)
@@ -345,10 +346,11 @@
             acc[pl.ds(rows_part * t, rows_part), :] += total
             if t + 1 == GRAM_PARTS:
                 ones = jnp.ones((16, NODES), jnp.bfloat16)
-                acc[TRI:GRAM_ROWS] += contract(ones, members[2 * h]) + contract(ones, members[2 * h + 1])
+                for side in range(SIDES):
+                    acc[TRI:GRAM_ROWS] += contract(ones, members[SIDES * h + side])
             return carry
 
-        lax.fori_loop(0, PLANES // 2, gram_planes, 0)
+        lax.fori_loop(0, PLANES // SIDES, gram_planes, 0)
         gram_copy(t).start()
 
     for t in range(GRAM_PARTS):
@@ -472,39 +474,56 @@
     packed_ref[...] = total
 
 
-def widen_kernel(received_ref, prolong_in, basis_ref, prolong_out, passing, in_sems, out_sems):
+def widen_kernel(
+    received_hbm, prolong_in, basis_hbm, prolong_out, received, basis, passing, received_sem, in_sems, out_sems,
+    basis_sems,
+):
+    received_copy = pltpu.make_async_copy(received_hbm, received, received_sem.at[0])
+    received_copy.start()
     part = PLANES // PASSES
-    inward, outward = [], []
+    inward, outward, basis_copies = [], [], []
     for i in range(PASSES):
         span = pl.ds(part * i, part)
         inward.append(pltpu.make_async_copy(prolong_in.at[span], passing.at[span], in_sems.at[i]))
         outward.append(pltpu.make_async_copy(passing.at[span], prolong_out.at[span], out_sems.at[i]))
     for copy in inward:
         copy.start()
-    pieces = split3(received_ref[...])
-    for m in range(K * K // WIDTH):
-        if m >= 2 and m - 2 < PASSES:
-            inward[m - 2].wait()
-            outward[m - 2].start()
+    blocks = K * K // WIDTH
+    places = {}
+    for m in range(2, blocks):
         group = m // 2
         width = K - 8 * group
         start = STARTS[8 * group]
         first = STARTS[4 * m] // WIDTH * WIDTH
         last = -(-(STARTS[4 * m] + 4 * width) // WIDTH) * WIDTH
-        if group == 0:
-            basis_ref[0, :, WIDTH * m : WIDTH * (m + 1)] = received_ref[:, first:last]
-            continue
         source = lax.broadcasted_iota(jnp.int32, (last - first, WIDTH), 0) + first
         column = lax.broadcasted_iota(jnp.int32, (last - first, WIDTH), 1) + WIDTH * m
         k, l = column // K, lax.rem(column, K)
         wanted = start + (k - 8 * group) * width + l - 8 * group
-        place = jnp.where(jnp.logical_and(source == wanted, l >= 8 * group), 1.0, 0.0).astype(jnp.bfloat16)
-        total = None
-        for piece in pieces:
-            term = jnp.dot(piece[:, first:last], place, preferred_element_type=jnp.float32)
-            total = term if total is None else total + term
-        basis_ref[0, :, WIDTH * m : WIDTH * (m + 1)] = total
-    for copy in outward:
+        places[m] = (
+            first,
+            last,
+            jnp.where(jnp.logical_and(source == wanted, l >= 8 * group), 1.0, 0.0).astype(jnp.bfloat16),
+        )
+    received_copy.wait()
+    for m in range(blocks):
+        lanes = pl.ds(WIDTH * m, WIDTH)
+        if m < 2:
+            basis[:, lanes] = received[:, lanes]
+        else:
+            first, last, place = places[m]
+            total = None
+            for piece in split3(received[:, first:last]):
+                term = jnp.dot(piece, place, preferred_element_type=jnp.float32)
+                total = term if total is None else total + term
+            basis[:, lanes] = total
+        copy = pltpu.make_async_copy(basis.at[:, lanes], basis_hbm.at[0, :, lanes], basis_sems.at[m])
+        copy.start()
+        basis_copies.append(copy)
+        if m < PASSES:
+            inward[m].wait()
+            outward[m].start()
+    for copy in outward + basis_copies:
         copy.wait()
 
 
@@ -553,7 +572,7 @@
             vmem((PLANES, ROWS, NODES), bf16),
             vmem((PLANES, 3, NODES, NODES), bf16),
             vmem((PLANES, WIDTH, NODES), bf16),
-            vmem((3, TRI // GRAM_PARTS, 2 * NODES), bf16),
+            vmem((3, TRI // GRAM_PARTS, SIDES * NODES), bf16),
             vmem((GRAM_ROWS, WIDTH)),
             vmem((GRAM_ROWS, WIDTH)),
             pltpu.SemaphoreType.DMA((2 * CHUNKS,)),
@@ -591,12 +610,16 @@
             jax.ShapeDtypeStruct((1, slots_total, K * K), jnp.float32),
             jax.ShapeDtypeStruct((PLANES, 4 * ROWS, 64), jnp.float32),
         ),
-        in_specs=[whole, any_spec],
-        out_specs=(whole, any_spec),
+        in_specs=[any_spec, any_spec],
+        out_specs=(any_spec, any_spec),
         scratch_shapes=[
+            vmem((slots_total, TRI)),
+            vmem((slots_total, K * K)),
             vmem((PLANES, 4 * ROWS, 64)),
+            pltpu.SemaphoreType.DMA((1,)),
             pltpu.SemaphoreType.DMA((PASSES,)),
             pltpu.SemaphoreType.DMA((PASSES,)),
+            pltpu.SemaphoreType.DMA((K * K // WIDTH,)),
         ],
         compiler_params=pltpu.CompilerParams(vmem_limit_bytes=57 * 1024 * 1024),
         name="widen",

time: 82.5 us -> 76.9 us (0.932)
  the two profiles are of different devices: /device:TPU:1 before, /device:TPU:0 now
where the time goes in v7:
time: 76.9 us; the launch traced here: 76.8 us
  Pallas kernels  76.2 us (99%)
    pallas_call x1, Pallas kernels, shards(): pl.pallas_call(functools.partial(setup_kernel, n_wide, n_narrow), out_sha...  72.2 us
    pallas_call x1, Pallas kernels, shards(): pl.pallas_call(widen_kernel, out_shape=(jax.ShapeDtypeStruct((1, slots_to...  3.95 us

profile of v7, /device:TPU:0, one launch (start us, length us, event | category | flops | bytes accessed | tf_op | source)
XLA Modules:
  0.0 76.8 jit_solution(2477328588480356525)
XLA Ops:
  0.6 72.2 %setup.1 = (f32[16,384,64]{2,1,0:T(8,128)}, f32[256,640]{1,0:T(8,128)}) custom-call(f32[16,384,64]{2,1,0:T(8,128)} %bitcast.10, f32[576,64]{1,0:T(8,128)} %bitcast.11, f32[384,64]{1,0:T(8,128)} %bitcast.12, f32[3,3,6]{2,1,0:T(4,128)} %bitcast.14, bf16[16,3,256,256]{3,2,1,0:T(8,128)(2,1)} %bitcast.9, s32[3,1,16]{2,1,0:T(1,128)} %bitcast.15, ...), custom_call_target="tpu_custom_call" | custom-call | tf_op jit(solution)/shard_map/setup/pallas_call | solution.py:543
  72.8 4.0 %widen.1 = (f32[1,256,1024]{2,1,0:T(8,128)}, f32[16,384,64]{2,1,0:T(8,128)}) custom-call(f32[256,640]{1,0:T(8,128)} %get-tuple-element.6.received_hbm, f32[16,384,64]{2,1,0:T(8,128)} %get-tuple-element.7.prolong_in), custom_call_target="tpu_custom_call" | custom-call | tf_op jit(solution)/shard_map/widen/pallas_call | solution.py:607

commit v8 on v7

--- a/solution.py
+++ b/solution.py
@@ -289,22 +289,26 @@
             sources[slot][col_ref[slot, 0, r]], tiles[r, slot], preferred_element_type=jnp.float32
         )
 
-    def near_far(r, carry):
-        comb_ref[r] = comb_ref[r] + far_product(r, 1)
-        return carry
-
-    lax.fori_loop(0, PLANES, near_far, 0)
+    def near_far(h, carry):
+        products = [far_product(SIDES * h + side, 1) for side in range(SIDES)]
+        for side in range(SIDES):
+            comb_ref[SIDES * h + side] = comb_ref[SIDES * h + side] + products[side]
+        return carry
+
+    lax.fori_loop(0, PLANES // SIDES, near_far, 0)
 
     acc[...] = jnp.zeros_like(acc)
     for q in range(CHUNKS):
         for copy in plane_copies(q):
             copy.wait()
 
-    def side_far(r, carry):
-        comb_ref[r] = comb_ref[r] + (far_product(r, 0) + far_product(r, 2))
-        return carry
-
-    lax.fori_loop(0, PLANES, side_far, 0)
+    def side_far(h, carry):
+        products = [far_product(SIDES * h + side, 0) + far_product(SIDES * h + side, 2) for side in range(SIDES)]
+        for side in range(SIDES):
+            comb_ref[SIDES * h + side] = comb_ref[SIDES * h + side] + products[side]
+        return carry
+
+    lax.fori_loop(0, PLANES // SIDES, side_far, 0)
 
     pairs = len(BLOCKS) // 2 // GRAM_PARTS
     rows_part = 16 * pairs

time: 76.9 us -> 75.4 us (0.980)
  the two profiles are of different devices: /device:TPU:0 before, /device:TPU:1 now
where the time goes in v8:
time: 75.4 us; the launch traced here: 74 us
  Pallas kernels  73.4 us (97%)
    pallas_call x1, Pallas kernels, shards(): pl.pallas_call(functools.partial(setup_kernel, n_wide, n_narrow), out_sha...  69.4 us
    pallas_call x1, Pallas kernels, shards(): pl.pallas_call(widen_kernel, out_shape=(jax.ShapeDtypeStruct((1, slots_to...  3.95 us

profile of v8, /device:TPU:1, one launch (start us, length us, event | category | flops | bytes accessed | tf_op | source)
XLA Modules:
  0.0 74.0 jit_solution(7962324502758046251)
XLA Ops:
  0.6 69.4 %setup.1 = (f32[16,384,64]{2,1,0:T(8,128)}, f32[256,640]{1,0:T(8,128)}) custom-call(f32[16,384,64]{2,1,0:T(8,128)} %bitcast.10, f32[576,64]{1,0:T(8,128)} %bitcast.11, f32[384,64]{1,0:T(8,128)} %bitcast.12, f32[3,3,6]{2,1,0:T(4,128)} %bitcast.14, bf16[16,3,256,256]{3,2,1,0:T(8,128)(2,1)} %bitcast.9, s32[3,1,16]{2,1,0:T(1,128)} %bitcast.15, ...), custom_call_target="tpu_custom_call" | custom-call | tf_op jit(solution)/shard_map/setup/pallas_call | solution.py:547
  70.0 4.0 %widen.1 = (f32[1,256,1024]{2,1,0:T(8,128)}, f32[16,384,64]{2,1,0:T(8,128)}) custom-call(f32[256,640]{1,0:T(8,128)} %get-tuple-element.6.received_hbm, f32[16,384,64]{2,1,0:T(8,128)} %get-tuple-element.7.prolong_in), custom_call_target="tpu_custom_call" | custom-call | tf_op jit(solution)/shard_map/widen/pallas_call | solution.py:611
